TPU v7x, 256 devices: a whole 4x4x8 slice. The times are simulated.
256 devices in a mesh: clip: 64 (over y, x_hi, z), proj: 4 (over x_lo, core).
Axes of the slice: x: 4 (x_hi: 2, x_lo: 2; x = x_hi * 2 + x_lo), y: 4, z: 8, core: 2. Of those that a mesh axis runs over, the one named last changes fastest.
Arguments:
- clip_acts: bfloat16 [512, 64, 768], P(('clip', 'proj')), may hold values from -6 to 6
- clip_cotangents: bfloat16 [512, 64, 768], P(('clip', 'proj')), may hold values from -6 to 6
- weight_in: bfloat16 [768, 3072], replicated, may hold values from -0.21875 to 0.21875
- weight_out: bfloat16 [3072, 768], replicated, may hold values from -0.21875 to 0.21875
- proj_in: bfloat16 [768, 32], replicated, may hold values from -0.21875 to 0.21875
- proj_out: bfloat16 [3072, 32], replicated, may hold values from -0.109375 to 0.109375
- test_grads: bfloat16 [512, 1024], P(('clip', 'proj')), may hold values from -6 to 6
- clip_ids: int32 [512], P(('clip', 'proj')), may hold values from 0 to 1, as said below
Outputs:
- scores: float32 [512, 512], P(('clip', 'proj'))
Inputs may be any that keep to these rules, and one draw needn't show every extreme that they name: `clip_ids`: in each aligned block of 2 entries (the clips of one device) every number from 0 to 1 stands once.
All inputs are finite; a program needn't handle non-finite values.
Results may differ from a plain program's by a relative error of at most 0.0065.
Values may be sent and summed in bfloat16 or wider, within the bound.
A program may use at most 128 MiB of HBM per device.

v0:
```python
import math

import jax
import jax.numpy as jnp
from jax import lax
from jax.sharding import PartitionSpec as P

damp_ratio = 0.1


def gelu_slope(values):
    normal_cdf = 0.5 * (1.0 + jax.scipy.special.erf(values / math.sqrt(2.0)))
    normal_pdf = jnp.exp(-0.5 * values * values) / math.sqrt(2.0 * math.pi)
    return normal_cdf + values * normal_pdf


def split_product(packed, exact, contract):
    upper = exact.astype(jnp.bfloat16)
    kept = lax.optimization_barrier(upper)
    lower = (exact - kept.astype(jnp.float32)).astype(jnp.bfloat16)
    first = lax.dot_general(packed, upper, contract, preferred_element_type=jnp.float32)
    second = lax.dot_general(packed, lower, contract, preferred_element_type=jnp.float32)
    return first + second


def body(
    clip_acts, clip_cotangents, weight_in, weight_out, proj_in, proj_out, test_grads, clip_ids
):
    clip_count, frame_count, feature_width = clip_acts.shape
    in_width = proj_in.shape[1]
    out_width = proj_out.shape[1]
    proj_width = in_width * out_width
    train_total = clip_count * lax.axis_size("clip") * lax.axis_size("proj")
    flattened = clip_acts.reshape(-1, feature_width)
    preact = jnp.dot(flattened, weight_in, preferred_element_type=jnp.float32)
    backprop = lax.dot_general(
        clip_cotangents.reshape(-1, feature_width),
        weight_out,
        (((1,), (1,)), ((), ())),
        preferred_element_type=jnp.float32,
    )
    deltas = (backprop * gelu_slope(preact)).astype(jnp.bfloat16)
    left_side = jnp.dot(flattened, proj_in, preferred_element_type=jnp.float32).reshape(
        clip_count, frame_count, in_width
    )
    right_side = jnp.dot(deltas, proj_out, preferred_element_type=jnp.float32).reshape(
        clip_count, frame_count, out_width
    )
    outer = jnp.einsum("ctr,cto->cro", left_side, right_side, precision=lax.Precision.HIGHEST)
    vectors = (outer / math.sqrt(frame_count)).reshape(clip_count, proj_width).astype(jnp.bfloat16)
    widened = vectors.astype(jnp.float32)
    square_total = lax.psum(jnp.sum(widened * widened), ("clip", "proj"))
    slab_rows = proj_width // lax.axis_size("proj")
    slab_start = lax.axis_index("proj") * slab_rows
    stored = lax.all_gather(vectors, "proj", axis=0, tiled=True)
    columns = lax.dynamic_slice_in_dim(stored, slab_start, slab_rows, 1)
    slab_term = lax.dot_general(
        columns, stored, (((0,), (0,)), ((), ())), preferred_element_type=jnp.float32
    )
    slab_sum = lax.psum(slab_term, "clip")
    gram_matrix = lax.all_gather(slab_sum, "proj", axis=0, tiled=True)
    gram_matrix = gram_matrix / train_total
    trace_value = square_total / train_total
    damping = damp_ratio * trace_value / proj_width
    system = gram_matrix + damping * jnp.eye(proj_width, dtype=jnp.float32)
    factor = jnp.linalg.cholesky(system)
    solved = jax.scipy.linalg.cho_solve((factor, True), test_grads.astype(jnp.float32).T)
    all_tests = lax.all_gather(solved.T, ("clip", "proj"), axis=0, tiled=True)
    raw = split_product(vectors, all_tests, (((1,), (1,)), ((), ())))
    raw = raw / math.sqrt(proj_width)
    return jnp.take(raw, clip_ids, axis=0)


def solution(mesh):
    in_specs = (
        P(("clip", "proj"), None, None),
        P(("clip", "proj"), None, None),
        P(),
        P(),
        P(),
        P(),
        P(("clip", "proj"), None),
        P(("clip", "proj")),
    )
    out_specs = P(("clip", "proj"), None)
    return jax.shard_map(body, mesh=mesh, in_specs=in_specs, out_specs=out_specs, check_vma=False)
```

profile of v0, /device:TPU:3, one launch (start us, length us, event | category | flops | bytes accessed | tf_op | source)
XLA Modules:
  0.0 1559.9 jit_solution(10206789239391568107)
XLA Ops:
  8.4 3.2 fusion.119
  11.6 3.9 fusion.6
  16.5 6.0 all-gather
  22.5 1.3 fusion.87
  23.9 649.3 %all-reduce.3.cloned.1.call-done = f32[256,1024]{0,1:T(8,128)} async-done(((f32[256,1024]{0,1:T(8,128)}), f32[256,1024]{0,1:T(8,128)}) %all-reduce.3.cloned.1.call-update) | async-done | bytes 1048592 | tf_op jit(solution)/shard_map/psum | solution.py:60
  673.3 121.2 %psum.15 = f32[]{:T(128)} all-reduce(f32[]{:T(128)} %get-tuple-element.62), channel_id=1, replica_groups=mesh['clip'=64,'proj'=4] {'clip','proj'}, use_global_device_ids=true, to_apply=%region_2.0 | all-reduce | flops 1 | bytes 8 | tf_op jit(solution)/shard_map/psum | solution.py:52
  795.1 5.0 select_add_fusion
  800.2 5.5 copy.30
  805.7 4.5 fusion
  810.2 1.9 copy-done.2
  812.1 11.7 cholesky.222
  823.9 9.8 custom-call.66
  833.8 1.5 fusion.22
  835.5 1.6 convolution_subtract_fusion
  837.1 11.7 cholesky.243
  849.1 9.8 custom-call.67
  860.0 2.0 copy-done.1
  862.0 2.4 convolution_subtract_fusion.1
  864.4 11.7 cholesky.466
  876.9 9.8 custom-call.68
  886.7 1.3 convolution_dynamic-update-slice_fusion.1
  888.0 3.5 convolution_subtract_fusion.2
  891.5 11.7 cholesky.485
  904.0 9.8 custom-call.69
  913.9 1.1 convolution_dynamic-update-slice_fusion.2
  915.0 3.1 convolution_subtract_fusion.3
  918.1 11.9 cholesky.504
  930.8 9.8 custom-call.70
  940.6 1.1 convolution_dynamic-update-slice_fusion.3
  941.7 3.1 convolution_subtract_fusion.4
  944.8 11.7 cholesky.524
  957.3 9.8 custom-call.71
  968.1 2.9 convolution_subtract_fusion.5
  971.0 11.7 cholesky.544
  983.5 9.8 custom-call.72
  994.2 2.1 convolution_subtract_fusion.6
  996.3 11.7 cholesky.562
  1018.4 4.8 select_select_fusion
  1023.2 23.9 %while.1 = (s32[]{:T(128)}, f32[1024,1024]{0,1:T(8,128)}, s32[8,2]{0,1:T(2,128)S(1)}, f32[8,128,128]{2,1,0:T(8,128)S(1)}, s32[]{:T(128)}) while((s32[]{:T(128)}, f32[1024,1024]{0,1:T(8,128)}, s32[8,2]{0,1:T(2,128)S(1)}, f32[8,128,128]{2,1,0:T(8,128)S(1)}, s32[]{:T(128)}) %tuple.51), condition=%wide.while_cond, body=%wide.while_body.sunk | while | flops 2 | bytes 393329 | solution.py:67
  1023.8 2.3 dynamic-slice.7
  1026.8 2.3 dynamic-slice.7
  1029.8 2.3 dynamic-slice.7
  1032.8 2.3 dynamic-slice.7
  1035.8 2.3 dynamic-slice.7
  1038.8 2.3 dynamic-slice.7
  1041.8 2.3 dynamic-slice.7
  1044.8 2.2 dynamic-slice.7
  1047.1 78.8 %custom-call.73 = f32[8,128,128]{1,2,0:T(8,128)S(1)} custom-call(f32[8,128,128]{2,1,0:T(8,128)S(1)} %get-tuple-element.12), custom_call_target="InvertDiagBlocksLowerTriangular" | custom-call | tf_op jit(solution)/shard_map/jit(_cho_solve)/triangular_solve | solution.py:67
  1126.1 1.0 convolution_subtract_fusion.12
  1127.3 1.1 convolution_subtract_fusion.8
  1128.6 1.2 convolution_subtract_fusion.20
  1129.9 1.2 convolution_subtract_fusion.18
  1131.3 1.3 convolution_subtract_fusion.17
  1132.8 1.3 convolution_subtract_fusion.11
  1134.3 1.4 convolution_subtract_fusion.16
  1136.2 1.1 convolution_subtract_fusion.10
  1137.5 1.1 convolution_subtract_fusion.7
  1138.8 1.2 convolution_subtract_fusion.19
  1140.3 1.3 convolution_subtract_fusion.15
  1141.9 1.4 convolution_subtract_fusion.14
  1143.5 1.4 convolution_subtract_fusion.9
  1145.2 1.5 convolution_subtract_fusion.13
  1147.8 400.2 %all-gather.7.cloned.1.call-done = f32[256,2,1024]{2,1,0:T(2,128)} async-done(((f32[1,2,1024]{2,1,0:T(2,128)}), f32[256,2,1024]{2,1,0:T(2,128)}) %all-gather.7.cloned.1.call-update) | async-done | bytes 2097168 | tf_op jit(solution)/shard_map/all_gather | solution.py:68
  1548.0 2.7 reshape.156
  (152 shorter events, 28.0 us)
Async XLA Ops:
  6.5 0.9 copy-start
  6.5 5.1 copy-start.5
  6.5 5.1 copy-start.6
  6.5 666.7 %all-reduce.3.cloned.1.call-start = ((), (), s32[]{:S(2)}) async-start(), calls=%async_computation | async-start | bytes 2097152 | tf_op jit(solution)/shard_map/psum | solution.py:60
  11.6 783.5 %copy-start.4 = (bf16[2,1024]{1,0:T(2,128)(2,1)S(1)}, bf16[2,1024]{1,0:T(2,128)(2,1)}, u32[]{:S(2)}) copy-start(bf16[2,1024]{1,0:T(2,128)(2,1)} %param.14) | copy-start | bytes 12292
  23.9 771.3 %all-gather.5.cloned.1.call-start = ((), (), s32[]{:S(2)}) async-start(), calls=%async_computation.1 | async-start | bytes 5242880 | tf_op jit(solution)/shard_map/all_gather | solution.py:61
  673.2 874.8 %all-gather.7.cloned.1.call-start = ((), (), s32[]{:S(2)}) async-start(), calls=%async_computation.2 | async-start | bytes 2105344 | tf_op jit(solution)/shard_map/all_gather | solution.py:68
  810.1 1.9 copy-start.2
  860.0 2.0 copy-start.1
  1023.2 124.6 %copy-start.7 = (s32[2]{0:T(128)S(1)}, s32[2]{0:T(128)}, u32[]{:S(2)}) copy-start(s32[2]{0:T(128)} %param.15) | copy-start | bytes 28
  1147.1 0.6 copy-start.3
Sparse Core Ops, SparseCore 0:
  24.0 649.1 all-reduce.2
  675.1 93.1 all-gather.4
  1147.8 400.1 all-gather.6
where the time goes:
time: 1570 us; the launch traced here: 1560 us
  waiting for transfers between devices  1050 us (67%)
  other arithmetic  261 us (17%)
  blocking collectives  127 us (8%)
  matrix products  57.8 us (4%)
  local copies, waits for them, and re-layouts  44 us (3%)
  between operations  19.7 us (1%)
    psum x1, waiting for transfers between devices, body(): slab_sum = lax.psum(slab_term, 'clip')  649 us
    all_gather x1, waiting for transfers between devices, body(): all_tests = lax.all_gather(solved.T, ('clip', 'proj'), axis=0, tiled=True)  400 us
    another operation x30, other arithmetic, body(): factor = jnp.linalg.cholesky(system)  167 us
    psum x1, blocking collectives, body(): square_total = lax.psum(jnp.sum(widened * widened), ('clip', 'proj'))  121 us
    another operation x3, other arithmetic, body(): jax.scipy.linalg.cho_solve((factor, True), test_grads.astype(jnp.float32).T)  83.7 us
  transfers between devices with their start and end apart: 3, of which 2 were waited for; matrix products, arithmetic and copies ran while one was open for 0% of the time, Pallas kernels for 0%

commit v1 on v0

v1 whole, which is shorter than its diff:
```python
import functools
import math

import jax
import jax.numpy as jnp
from jax import lax
from jax.experimental import pallas as pl
from jax.experimental.pallas import tpu as pltpu
from jax.sharding import PartitionSpec as P

MESH = pl.DeviceIdType.MESH
F32, BF16 = jnp.float32, jnp.bfloat16
damp_ratio = 0.1

NY, NX, NZ, XLO = 4, 4, 8, 2
PLANE = NY * NX
TILE = 16
ROWS = 2 * NZ
TOLERANCE = 1e-6
MOST_STEPS = 4096


def gelu_slope(values):
    normal_cdf = 0.5 * (1.0 + jax.scipy.special.erf(values / math.sqrt(2.0)))
    normal_pdf = jnp.exp(-0.5 * values * values) / math.sqrt(2.0 * math.pi)
    return normal_cdf + values * normal_pdf


def my_place():
    clip, proj = lax.axis_index("clip"), lax.axis_index("proj")
    xh = NX // XLO
    y, z = clip // (xh * NZ), lax.rem(clip, NZ)
    x = lax.rem(clip // NZ, xh) * XLO + proj // 2
    return y, x, z, lax.rem(proj, 2)


def device_at(y, x, z, core):
    return {
        "clip": (y * (NX // XLO) + x // XLO) * NZ + z,
        "proj": lax.rem(x, XLO) * 2 + core,
    }


PLANE_STEPS = sorted(
    ((dy, dx) for dy in range(NY) for dx in range(NX) if (dy, dx) != (0, 0)),
    key=lambda s: min(s[0], NY - s[0]) + min(s[1], NX - s[1]),
)


def gather_kernel(
    v_ref, t_ref, v_all, t_all, line, wide, z_send, z_recv, p_send, p_recv, c_send, c_recv
):
    y, x, z, core = my_place()
    other = 1 - core
    chunks = v_all.shape[1] // 128
    half = PLANE * ROWS

    def along_z(d):
        return lax.rem(z + d, NZ)

    def in_plane(step):
        return lax.rem(y + step[0], NY), lax.rem(x + step[1], NX)

    barrier = pltpu.get_barrier_semaphore()
    targets = [device_at(y, x, along_z(d), core) for d in range(1, NZ)]
    targets += [device_at(*in_plane(s), z, core) for s in PLANE_STEPS]
    targets += [device_at(y, x, z, other)]
    for target in targets:
        pl.semaphore_signal(barrier, inc=1, device_id=target, device_id_type=MESH)
    pl.semaphore_wait(barrier, len(targets))

    def rows_of(place, of_core):
        start = of_core * half + (place[0] * NX + place[1]) * ROWS
        return pl.ds(pl.multiple_of(start, ROWS), ROWS)

    def z_copy(a, d, src, slot):
        return pltpu.make_async_remote_copy(
            src_ref=src,
            dst_ref=line.at[a, slot],
            send_sem=z_send.at[a, d - 1],
            recv_sem=z_recv.at[a, d - 1],
            device_id=targets[d - 1],
            device_id_type=MESH,
        )

    def p_copy(a, k, full, place):
        block = full.at[rows_of(place, core)]
        return pltpu.make_async_remote_copy(
            src_ref=block,
            dst_ref=block,
            send_sem=p_send.at[a, k],
            recv_sem=p_recv.at[a, k],
            device_id=targets[NZ - 1 + k],
            device_id_type=MESH,
        )

    def c_copy(a, k, full, place, of_core):
        block = full.at[rows_of(place, of_core)]
        return pltpu.make_async_remote_copy(
            src_ref=block,
            dst_ref=block,
            send_sem=c_send.at[a, k],
            recv_sem=c_recv.at[a, k],
            device_id=targets[-1],
            device_id_type=MESH,
        )

    fulls = (v_all, t_all)
    sources = (v_ref, t_ref)
    for a in range(2):
        for d in range(1, NZ):
            z_copy(a, d, sources[a], z).start()
        line[a, z] = sources[a][...]
    back = [(NY - s[0], NX - s[1]) for s in PLANE_STEPS]
    for a in range(2):
        full = fulls[a]
        for d in range(1, NZ):
            z_copy(a, d, sources[a], lax.rem(z + NZ - d, NZ)).wait_recv()
        wide[...] = line[a].reshape(NZ * TILE, 128).astype(F32)
        mine = rows_of((y, x), core)
        for c in range(chunks):
            full[mine, c * 128 : (c + 1) * 128] = wide[pl.ds(c, ROWS, stride=chunks), :].astype(
                BF16
            )
        for k in range(len(PLANE_STEPS)):
            p_copy(a, k, full, (y, x)).start()
        c_copy(a, 0, full, (y, x), core).start()
    for a in range(2):
        full = fulls[a]
        for k, s in enumerate(back):
            p_copy(a, k, full, in_plane(s)).wait_recv()
            c_copy(a, k + 1, full, in_plane(s), core).start()
    for a in range(2):
        full = fulls[a]
        for k, s in enumerate([(0, 0)] + back):
            c_copy(a, k, full, in_plane(s), other).wait_recv()
        for d in range(1, NZ):
            z_copy(a, d, sources[a], z).wait_send()
        for k, s in enumerate(PLANE_STEPS):
            p_copy(a, k, full, (y, x)).wait_send()
        for k, s in enumerate([(0, 0)] + back):
            c_copy(a, k, full, in_plane(s), core).wait_send()


def gather(v_tile, t_tile, width):
    everyone = 2 * PLANE * ROWS
    steps = len(PLANE_STEPS)
    full = jax.ShapeDtypeStruct((everyone, width), BF16)
    vmem = pl.BlockSpec(memory_space=pltpu.VMEM)
    dma = pltpu.SemaphoreType.DMA
    return pl.pallas_call(
        gather_kernel,
        out_shape=(full, full),
        in_specs=[vmem, vmem],
        out_specs=(vmem, vmem),
        scratch_shapes=[
            pltpu.VMEM((2, NZ, TILE, 128), BF16),
            pltpu.VMEM((NZ * TILE, 128), F32),
            dma((2, NZ - 1)),
            dma((2, NZ - 1)),
            dma((2, steps)),
            dma((2, steps)),
            dma((2, steps + 1)),
            dma((2, steps + 1)),
        ],
        compiler_params=pltpu.CompilerParams(
            collective_id=0, has_side_effects=True, vmem_limit_bytes=32 << 20
        ),
    )(v_tile, t_tile)


def pieces(values):
    first = values.astype(BF16).astype(F32)
    rest = values - first
    second = rest.astype(BF16).astype(F32)
    return first, second, rest - second


def stacked(values):
    first, second, third = pieces(values)
    return jnp.concatenate([first, second, third, jnp.zeros_like(first)], axis=0).astype(BF16)


def unstacked(product):
    return product[0:8] + product[8:16] + product[16:24]


def solve_kernel(ids_ref, v_ref, t_ref, out_ref, k_ref, split_ref):
    y, x, z, core = my_place()
    count, width = v_ref.shape
    gram = lax.dot_general(
        v_ref[...], v_ref[...], (((1,), (1,)), ((), ())), preferred_element_type=F32
    )
    gram = gram / count
    row = lax.broadcasted_iota(jnp.int32, (count, count), 0)
    column = lax.broadcasted_iota(jnp.int32, (count, count), 1)
    diagonal = jnp.sum(jnp.where(row == column, gram, 0.0), axis=0, keepdims=True)
    damping = damp_ratio * jnp.sum(diagonal, axis=1, keepdims=True) / width
    k_ref[...] = gram + jnp.where(row == column, damping, 0.0)
    diagonal = diagonal + damping
    first, second, third = pieces(k_ref[...])
    split_ref[:, 0:count] = first.astype(BF16)
    split_ref[:, count : 2 * count] = second.astype(BF16)
    split_ref[:, 2 * count : 3 * count] = third.astype(BF16)

    def times_system(p):
        product = unstacked(jnp.dot(stacked(p), split_ref[...], preferred_element_type=F32))
        return (
            product[:, 0:count]
            + product[:, count : 2 * count]
            + product[:, 2 * count : 3 * count]
        )

    def inner(a, b):
        return jnp.sum(a * b, axis=1, keepdims=True)

    def ratio(a, b):
        return jnp.where(b > 0.0, a / jnp.where(b > 0.0, b, 1.0), 0.0)

    base = core * (PLANE * ROWS) + (y * NX + x) * ROWS + z * 2
    lane = lax.broadcasted_iota(jnp.int32, (8, count), 1)
    sub = lax.broadcasted_iota(jnp.int32, (8, count), 0)
    wanted = jnp.where(sub == 0, base + ids_ref[0], base + ids_ref[1])
    rhs = jnp.where((lane == wanted) & (sub < 2), 1.0, 0.0)

    scale = 1.0 / diagonal
    zed = rhs * scale
    rz = inner(rhs, zed)
    goal = rz * (TOLERANCE * TOLERANCE)

    def unfinished(state):
        step, _, _, _, rz = state
        return (step < MOST_STEPS) & (jnp.max(rz - goal) > 0.0)

    def advance(state):
        step, sol, res, p, rz = state
        q = times_system(p)
        alpha = ratio(rz, inner(p, q))
        sol = sol + alpha * p
        res = res - alpha * q
        zed = res * scale
        new = inner(res, zed)
        p = zed + ratio(new, rz) * p
        return step + 1, sol, res, p, new

    state = (jnp.int32(0), jnp.zeros_like(rhs), rhs, zed, rz)
    sol = lax.while_loop(unfinished, advance, state)[1]

    mixed = unstacked(jnp.dot(stacked(sol), v_ref[...], preferred_element_type=F32))
    raw = unstacked(
        lax.dot_general(
            stacked(mixed), t_ref[...], (((1,), (1,)), ((), ())), preferred_element_type=F32
        )
    )
    raw = raw / math.sqrt(width)
    t_core, t_rest = row // (PLANE * ROWS), lax.rem(row, PLANE * ROWS)
    t_y, t_x = t_rest // (NX * ROWS), lax.rem(t_rest // ROWS, NX)
    t_z, t_k = lax.rem(t_rest, ROWS) // 2, lax.rem(t_rest, 2)
    goes = ((t_y * (NX // XLO) + t_x // XLO) * NZ + t_z) * (4 * XLO)
    goes = goes + (lax.rem(t_x, XLO) * 2 + t_core) * 2 + t_k
    order = jnp.where(goes == column, 1.0, 0.0).astype(BF16)
    raw = unstacked(jnp.dot(stacked(raw), order, preferred_element_type=F32))
    out_ref[...] = raw[0:2]


def solve(clip_ids, v_all, t_all):
    count = v_all.shape[0]
    vmem = pl.BlockSpec(memory_space=pltpu.VMEM)
    return pl.pallas_call(
        solve_kernel,
        out_shape=jax.ShapeDtypeStruct((2, count), F32),
        in_specs=[pl.BlockSpec(memory_space=pltpu.SMEM), vmem, vmem],
        out_specs=vmem,
        scratch_shapes=[
            pltpu.VMEM((count, count), F32),
            pltpu.VMEM((count, 3 * count), BF16),
        ],
        compiler_params=pltpu.CompilerParams(vmem_limit_bytes=48 << 20),
    )(clip_ids, v_all, t_all)


def body(
    clip_acts, clip_cotangents, weight_in, weight_out, proj_in, proj_out, test_grads, clip_ids
):
    clip_count, frame_count, feature_width = clip_acts.shape
    in_width = proj_in.shape[1]
    out_width = proj_out.shape[1]
    proj_width = in_width * out_width
    flattened = clip_acts.reshape(-1, feature_width)
    preact = jnp.dot(flattened, weight_in, preferred_element_type=F32)
    backprop = lax.dot_general(
        clip_cotangents.reshape(-1, feature_width),
        weight_out,
        (((1,), (1,)), ((), ())),
        preferred_element_type=F32,
    )
    deltas = (backprop * gelu_slope(preact)).astype(BF16)
    left_side = jnp.dot(flattened, proj_in, preferred_element_type=F32).reshape(
        clip_count, frame_count, in_width
    )
    right_side = jnp.dot(deltas, proj_out, preferred_element_type=F32).reshape(
        clip_count, frame_count, out_width
    )
    outer = jnp.einsum("ctr,cto->cro", left_side, right_side, precision=lax.Precision.HIGHEST)
    vectors = (outer / math.sqrt(frame_count)).astype(BF16)
    v_all, t_all = gather(
        vectors.reshape(TILE, 128), test_grads.reshape(TILE, 128), proj_width
    )
    return solve(clip_ids, v_all, t_all)


def solution(mesh):
    in_specs = (
        P(("clip", "proj"), None, None),
        P(("clip", "proj"), None, None),
        P(),
        P(),
        P(),
        P(),
        P(("clip", "proj"), None),
        P(("clip", "proj")),
    )
    out_specs = P(("clip", "proj"), None)
    return jax.shard_map(body, mesh=mesh, in_specs=in_specs, out_specs=out_specs, check_vma=False)
```

time: 1570 us -> 69.9 us (0.04)
  the two profiles are of different devices: /device:TPU:3 before, /device:TPU:1 now
where the time goes in v1:
time: 69.9 us; the launch traced here: 69.7 us
  Pallas kernels  59.6 us (85%)
  matrix products  8.25 us (12%)
  local copies, waits for them, and re-layouts  1.82 us (3%)
    pallas_call x1, Pallas kernels, gather(): pl.pallas_call(gather_kernel, out_shape=(full, full), in_specs=[vmem, vme...  31.2 us
    pallas_call x1, Pallas kernels, solve(): pl.pallas_call(solve_kernel, out_shape=jax.ShapeDtypeStruct((2, count), F...  28.3 us
    dot_general x1, matrix products, body(): jnp.dot(deltas, proj_out, preferred_element_type=F32)  3.91 us
    dot_general x1, matrix products, body(): preact = jnp.dot(flattened, weight_in, preferred_element_type=F32)  3.21 us

profile of v1, /device:TPU:1, one launch (start us, length us, event | category | flops | bytes accessed | tf_op | source)
XLA Modules:
  0.0 69.7 jit_solution(17532428395472398282)
XLA Ops:
  0.0 0.0 copy-start
  0.0 0.9 %copy-done = bf16[2,64,768]{2,1,0:T(8,128)(2,1)S(1)} copy-done((bf16[2,64,768]{2,1,0:T(8,128)(2,1)S(1)}, bf16[2,64,768]{2,1,0:T(8,128)(2,1)}, u32[]{:S(2)}) %copy-start) | copy-done | bytes 196632
  0.9 0.7 reshape.22.t_ref
  1.6 1.0 %fusion.12 = f32[2,64,32]{1,2,0:T(8,128)S(1)} fusion(bf16[2,64,768]{2,1,0:T(8,128)(2,1)S(1)} %copy-done, bf16[768,32]{0,1:T(8,128)(2,1)} %param.12), kind=kOutput, calls=%fused_computation.15 | convolution fusion | flops 6291456 | bytes 262144 | tf_op jit(solution)/shard_map/dot_general | solution.py:298
  2.6 0.0 copy-start.2
  2.6 0.0 copy-start.3
  2.6 3.2 %fusion.20 = f32[128,3072]{1,0:T(8,128)S(1)} fusion(bf16[128,768]{1,0:T(8,128)(2,1)S(1)} %bitcast.14, bf16[768,3072]{1,0:T(8,128)(2,1)} %param.10), kind=kOutput, calls=%fused_computation.23 | convolution fusion | flops 603979776 | bytes 6488064 | tf_op jit(solution)/shard_map/dot_general | solution.py:290
  5.8 0.0 copy-done.2
  5.8 0.0 copy-done.3
  5.9 0.0 copy-start.1
  5.9 3.9 %fusion.5 = f32[128,32]{0,1:T(8,128)S(1)} fusion(bf16[3072,32]{0,1:T(8,128)(2,1)S(1)} %copy-done.2, bf16[128,768]{1,0:T(8,128)(2,1)S(1)} %bitcast.15, bf16[3072,768]{1,0:T(8,128)(2,1)} %param.11, f32[128,3072]{1,0:T(8,128)S(1)} %fusion.20), kind=kOutput, calls=%fused_computation.7 | convolution fusion | flops 633077760 | bytes 6701056 | tf_op jit(solution)/shard_map/dot_general | solution.py:301
  9.8 0.1 reshape.20
  9.9 0.2 fusion.6
  10.1 0.1 reshape.21.v_ref
  10.1 31.2 %shard_map.82 = (bf16[512,1024]{1,0:T(8,128)(2,1)S(1)}, bf16[512,1024]{1,0:T(8,128)(2,1)S(1)}) custom-call(bf16[16,128]{1,0:T(8,128)(2,1)S(1)} %reshape.21.v_ref, bf16[16,128]{1,0:T(8,128)(2,1)S(1)} %reshape.22.t_ref), custom_call_target="tpu_custom_call" | custom-call | tf_op jit(solution)/shard_map/pallas_call | solution.py:151
  41.4 0.0 copy-done.1
  41.4 28.3 %shard_map.83 = f32[2,512]{1,0:T(2,128)} custom-call(s32[2]{0:T(128)S(1)} %copy-done.1, bf16[512,1024]{1,0:T(8,128)(2,1)S(1)} %get-tuple-element.7.v_ref, bf16[512,1024]{1,0:T(8,128)(2,1)S(1)} %get-tuple-element.8.t_ref), custom_call_target="tpu_custom_call" | custom-call | tf_op jit(solution)/shard_map/pallas_call | solution.py:269
Async XLA Ops:
  0.0 0.9 %copy-start = (bf16[2,64,768]{2,1,0:T(8,128)(2,1)S(1)}, bf16[2,64,768]{2,1,0:T(8,128)(2,1)}, u32[]{:S(2)}) copy-start(bf16[2,64,768]{2,1,0:T(8,128)(2,1)} %param.8) | copy-start | bytes 589828
  2.6 3.2 %copy-start.2 = (bf16[3072,32]{0,1:T(8,128)(2,1)S(1)}, bf16[3072,32]{0,1:T(8,128)(2,1)}, u32[]{:S(2)}) copy-start(bf16[3072,32]{0,1:T(8,128)(2,1)} %param.13) | copy-start | bytes 589828
  2.6 3.2 %copy-start.3 = (bf16[2,64,768]{2,1,0:T(8,128)(2,1)S(1)}, bf16[2,64,768]{2,1,0:T(8,128)(2,1)}, u32[]{:S(2)}) copy-start(bf16[2,64,768]{2,1,0:T(8,128)(2,1)} %param.9) | copy-start | bytes 589828
  5.9 35.5 %copy-start.1 = (s32[2]{0:T(128)S(1)}, s32[2]{0:T(128)}, u32[]{:S(2)}) copy-start(s32[2]{0:T(128)} %ids_ref.1) | copy-start | bytes 28

commit v2 on v0

v2 whole, which is shorter than its diff:
```python
import functools
import math

import jax
import jax.numpy as jnp
from jax import lax
from jax.experimental import pallas as pl
from jax.experimental.pallas import tpu as pltpu
from jax.sharding import PartitionSpec as P

MESH = pl.DeviceIdType.MESH
F32, BF16 = jnp.float32, jnp.bfloat16
damp_ratio = 0.1

NY, NX, NZ, XLO = 4, 4, 8, 2
PLANE = NY * NX
TILE = 16
ROWS = 2 * NZ
HALF = PLANE * ROWS
PARTS = 6
DOUBLINGS = 4
REFINEMENTS = 3
MOST_STEPS = 4096
LAST_BITS = 2.0**-22

PLANE_STEPS = sorted(
    ((dy, dx) for dy in range(NY) for dx in range(NX) if (dy, dx) != (0, 0)),
    key=lambda s: min(s[0], NY - s[0]) + min(s[1], NX - s[1]),
)
STEPS = len(PLANE_STEPS)
BACK = [(NY - s[0], NX - s[1]) for s in PLANE_STEPS]


def gelu_slope(values):
    normal_cdf = 0.5 * (1.0 + lax.erf(values * math.sqrt(0.5)))
    normal_pdf = jnp.exp(-0.5 * values * values) * (1.0 / math.sqrt(2.0 * math.pi))
    return normal_cdf + values * normal_pdf


def my_place():
    clip, proj = lax.axis_index("clip"), lax.axis_index("proj")
    xh = NX // XLO
    y, z = clip // (xh * NZ), lax.rem(clip, NZ)
    x = lax.rem(clip // NZ, xh) * XLO + proj // 2
    return y, x, z, lax.rem(proj, 2)


def device_at(y, x, z, core):
    return {
        "clip": (y * (NX // XLO) + x // XLO) * NZ + z,
        "proj": lax.rem(x, XLO) * 2 + core,
    }


def mm(a, b):
    return jnp.dot(a, b, preferred_element_type=F32)


def mm_t(a, b):
    return lax.dot_general(a, b, (((1,), (1,)), ((), ())), preferred_element_type=F32)


def pieces(values):
    first = values.astype(BF16).astype(F32)
    rest = values - first
    second = rest.astype(BF16).astype(F32)
    return first, second, rest - second


def stacked(values):
    first, second, third = pieces(values)
    return jnp.concatenate([first, second, third, jnp.zeros_like(first)], axis=0).astype(BF16)


def unstacked(product):
    return product[0:8] + product[8:16] + product[16:24]


def iota(shape, axis):
    return lax.broadcasted_iota(jnp.int32, shape, axis)


def inner(a, b):
    return jnp.sum(a * b, axis=1, keepdims=True)


def spread(ref, values):
    chunks = values.shape[1] // 128
    for c in range(chunks):
        ref[pl.ds(c, 2, stride=chunks), :] = values[:, c * 128 : (c + 1) * 128]
    return ref[...].astype(BF16)


def left_pieces(acts, proj_in):
    tokens, width = acts.shape[0], proj_in.shape[1]
    r, c = iota((width, 128), 0), iota((width, 128), 1)
    groups = 128 // width
    per = width // groups
    chosen = (c < width) & (r == lax.rem(c, per) * groups + c // per)
    ordered = mm(proj_in, jnp.where(chosen, 1.0, 0.0).astype(BF16)).astype(BF16)
    left = jnp.transpose(mm(acts, ordered))
    half = tokens // 2
    rows = []
    for k in range(2):
        lane = iota((per, tokens), 1)
        own = (lane >= k * half) & (lane < (k + 1) * half)
        row = [jnp.where(own, left[j * per : (j + 1) * per], 0.0) for j in range(groups)]
        rows.append(jnp.concatenate(row, axis=1))
    return jnp.concatenate(pieces(jnp.concatenate(rows, axis=0)), axis=0).astype(BF16)


def outer_tile(left, right, in_width):
    width = right.shape[1]
    groups = 128 // width
    wide = jnp.concatenate([right] * groups, axis=1)
    lane = iota(wide.shape, 1) // width
    stack = []
    for piece in pieces(wide):
        masked = [jnp.where(lane == j, piece, 0.0) for j in range(groups)]
        stack.append(jnp.concatenate(masked, axis=0).astype(BF16))
    product = mm(left, jnp.concatenate(stack, axis=1))
    total = None
    for i in (2, 1, 0):
        for j in (2, 1, 0):
            term = product[i * TILE : (i + 1) * TILE, j * 128 : (j + 1) * 128]
            total = term if total is None else total + term
    return total


def target_order(shape):
    j = iota((1, shape[1]), 1)
    k, core = lax.rem(j, 2), lax.rem(j // 2, 2)
    x_lo, z = lax.rem(j // 4, XLO), lax.rem(j // (4 * XLO), NZ)
    rest = j // (4 * XLO * NZ)
    x_hi, y = lax.rem(rest, NX // XLO), rest // (NX // XLO)
    source = core * HALF + (y * NX + x_hi * XLO + x_lo) * ROWS + z * 2 + k
    return jnp.where(iota(shape, 0) == source, 1.0, 0.0).astype(BF16)


def wanted_rows(ids_ref, count):
    y, x, z, core = my_place()
    base = core * HALF + (y * NX + x) * ROWS + z * 2
    lane, sub = iota((8, count), 1), iota((8, count), 0)
    wanted = jnp.where(sub == 0, base + ids_ref[0], base + ids_ref[1])
    return jnp.where((lane == wanted) & (sub < 2), 1.0, 0.0)


def form_system(v, split_ref):
    count, width = v.shape
    gram = mm_t(v, v) * (1.0 / count)
    eye = iota((count, count), 0) == iota((count, count), 1)
    diagonal = jnp.sum(jnp.where(eye, gram, 0.0), axis=0, keepdims=True)
    damping = damp_ratio * jnp.sum(diagonal, axis=1, keepdims=True) / width
    system = gram + jnp.where(eye, damping, 0.0)
    for i, piece in enumerate(pieces(system)):
        split_ref[:, i * count : (i + 1) * count] = piece.astype(BF16)
    return system, damping, diagonal + damping, eye


def times_system(p, split_ref):
    count = split_ref.shape[0]
    product = unstacked(mm(stacked(p), split_ref[...]))
    return (
        product[:, 0:count] + product[:, count : 2 * count] + product[:, 2 * count : 3 * count]
    )


def scores_of(sol, v, t):
    mixed = unstacked(mm(stacked(sol), v))
    raw = unstacked(mm_t(stacked(mixed), t)) * (1.0 / math.sqrt(v.shape[1]))
    return unstacked(mm(stacked(raw), target_order((t.shape[0], t.shape[0]))))


def refined(ids_ref, v, split_ref, m_ref):
    count = v.shape[0]
    system, low, _, eye = form_system(v, split_ref)
    high = split_ref[:, 0:count]
    square = mm(high, high)
    top = jnp.max(jnp.sum(jnp.abs(square), axis=0, keepdims=True), axis=1, keepdims=True)
    top = jnp.sqrt(top) * 1.02
    centre = 2.0 / (top + low)
    t = (top + low) / (top - low)
    t2 = 2.0 * t * t - 1.0
    c = 2.0 * t * t / t2 * centre
    m = jnp.where(eye, 2.0 * c, 0.0) - (c * centre) * system
    am = (2.0 * c) * system - (c * centre) * square
    for i in range(DOUBLINGS):
        t = t2
        t2 = 2.0 * t * t - 1.0
        c = 2.0 * t * t / t2
        rounded = m.astype(BF16)
        if i > 0:
            am = mm(high, rounded)
        m = c * (2.0 * m - mm(rounded, am.astype(BF16)))
    m_ref[...] = m.astype(BF16)

    rhs = wanted_rows(ids_ref, count)

    def precondition(r):
        return mm(jnp.concatenate([r, jnp.zeros_like(r)], axis=0).astype(BF16), m_ref[...])[0:8]

    sol = precondition(rhs)
    res = rhs - times_system(sol, split_ref)
    for _ in range(REFINEMENTS):
        sol = sol + precondition(res)
        res = rhs - times_system(sol, split_ref)
    excess = inner(res, res) - (LAST_BITS * top) * (LAST_BITS * top) * inner(sol, sol)
    return sol, excess


def main_kernel(
    ids_ref, acts_hbm, cot_hbm, w_in_hbm, w_out_hbm, proj_in_hbm, proj_out_hbm, t_ref,
    raw_ref, check_ref, v_out, t_out,
    acts, cot, w_in, w_out, proj_in, proj_out, v_all, t_all, tiles, line, wide, split_ref, m_ref,
    load_sem, in_sem, out_sem, store_sem, z_send, z_recv, p_send, p_recv, c_send, c_recv,
):
    y, x, z, core = my_place()
    other = 1 - core
    chunks = v_all.shape[1] // 128
    block = w_in.shape[1] // PARTS
    tokens = acts.shape[0] * acts.shape[1]

    small = [
        pltpu.make_async_copy(src, dst, load_sem.at[i])
        for i, (src, dst) in enumerate(
            ((acts_hbm, acts), (proj_in_hbm, proj_in), (cot_hbm, cot), (proj_out_hbm, proj_out))
        )
    ]
    loads_in, loads_out = [], []
    for i in range(PARTS):
        part = pl.ds(i * block, block)
        loads_in.append(
            pltpu.make_async_copy(w_in_hbm.at[:, part], w_in.at[:, part], in_sem.at[i])
        )
        loads_out.append(
            pltpu.make_async_copy(w_out_hbm.at[part], w_out.at[part], out_sem.at[i])
        )
    small[0].start()
    small[1].start()
    loads_in[0].start()
    small[2].start()
    loads_out[0].start()
    small[3].start()
    for i in range(1, PARTS):
        loads_in[i].start()
        loads_out[i].start()

    def along_z(d):
        return lax.rem(z + d, NZ)

    def in_plane(step):
        return lax.rem(y + step[0], NY), lax.rem(x + step[1], NX)

    barrier = pltpu.get_barrier_semaphore()
    targets = [device_at(y, x, along_z(d), core) for d in range(1, NZ)]
    targets += [device_at(*in_plane(s), z, core) for s in PLANE_STEPS]
    targets += [device_at(y, x, z, other)]
    for target in targets:
        pl.semaphore_signal(barrier, inc=1, device_id=target, device_id_type=MESH)

    def rows_of(place, of_core):
        start = of_core * HALF + (place[0] * NX + place[1]) * ROWS
        return pl.ds(pl.multiple_of(start, ROWS), ROWS)

    def z_copy(a, d, slot):
        return pltpu.make_async_remote_copy(
            src_ref=tiles.at[a],
            dst_ref=line.at[a, slot],
            send_sem=z_send.at[a, d - 1],
            recv_sem=z_recv.at[a, d - 1],
            device_id=targets[d - 1],
            device_id_type=MESH,
        )

    fulls = (v_all, t_all)

    def p_copy(a, k, place):
        rows = fulls[a].at[rows_of(place, core)]
        return pltpu.make_async_remote_copy(
            src_ref=rows,
            dst_ref=rows,
            send_sem=p_send.at[a, k],
            recv_sem=p_recv.at[a, k],
            device_id=targets[NZ - 1 + k],
            device_id_type=MESH,
        )

    def c_copy(a, k, place, of_core):
        rows = fulls[a].at[rows_of(place, of_core)]
        return pltpu.make_async_remote_copy(
            src_ref=rows,
            dst_ref=rows,
            send_sem=c_send.at[a, k],
            recv_sem=c_recv.at[a, k],
            device_id=targets[-1],
            device_id_type=MESH,
        )

    def start_line(a, tile):
        tiles[a] = tile
        for d in range(1, NZ):
            z_copy(a, d, z).start()
        line[a, z] = tile

    def start_plane(a):
        for d in range(1, NZ):
            z_copy(a, d, lax.rem(z + NZ - d, NZ)).wait_recv()
        wide[...] = line[a].reshape(NZ * TILE, 128).astype(F32)
        mine = rows_of((y, x), core)
        for c in range(chunks):
            fulls[a][mine, c * 128 : (c + 1) * 128] = wide[
                pl.ds(c, ROWS, stride=chunks), :
            ].astype(BF16)
        for k in range(STEPS):
            p_copy(a, k, (y, x)).start()
        c_copy(a, 0, (y, x), core).start()

    def forward(a):
        for k, s in enumerate(BACK):
            p_copy(a, k, in_plane(s)).wait_recv()
            c_copy(a, k + 1, in_plane(s), core).start()

    def finish(a):
        for k, s in enumerate([(0, 0)] + BACK):
            c_copy(a, k, in_plane(s), other).wait_recv()

    def settle(a):
        for d in range(1, NZ):
            z_copy(a, d, z).wait_send()
        for k in range(STEPS):
            p_copy(a, k, (y, x)).wait_send()
        for k, s in enumerate([(0, 0)] + BACK):
            c_copy(a, k, in_plane(s), core).wait_send()

    t_tile = spread(wide.at[pl.ds(0, TILE)], t_ref[...].astype(F32))
    pl.semaphore_wait(barrier, len(targets))
    start_line(1, t_tile)

    small[0].wait()
    small[1].wait()
    left = left_pieces(acts[...].reshape(tokens, -1), proj_in[...])
    small[2].wait()
    small[3].wait()
    right = None
    for i in range(PARTS):
        loads_in[i].wait()
        loads_out[i].wait()
        part = slice(i * block, (i + 1) * block)
        preact = mm(acts[...].reshape(tokens, -1), w_in[:, part])
        backprop = mm_t(cot[...].reshape(tokens, -1), w_out[part])
        deltas = (backprop * gelu_slope(preact)).astype(BF16)
        term = mm(deltas, proj_out[part])
        right = term if right is None else right + term
        if i == 1:
            start_plane(1)
    outer = outer_tile(left, right, proj_in.shape[1])
    start_line(0, (outer * (1.0 / math.sqrt(acts.shape[1]))).astype(BF16))
    forward(1)
    start_plane(0)
    finish(1)
    store_t = pltpu.make_async_copy(t_all, t_out, store_sem.at[1])
    store_t.start()
    forward(0)
    finish(0)
    store_v = pltpu.make_async_copy(v_all, v_out, store_sem.at[0])
    store_v.start()

    sol, excess = refined(ids_ref, v_all[...], split_ref, m_ref)
    raw_ref[...] = scores_of(sol, v_all[...], t_all[...])
    check_ref[...] = jnp.broadcast_to(excess, check_ref.shape)
    settle(1)
    settle(0)
    store_t.wait()
    store_v.wait()


def finish_kernel(ids_ref, raw_ref, check_ref, v_hbm, t_hbm, out_ref, v_ref, t_ref, split_ref, sem):
    out_ref[...] = raw_ref[0:2]
    excess = check_ref[...]
    fine = jnp.min(jnp.where(excess <= 0.0, 1.0, 0.0))

    @pl.when(fine < 1.0)
    def _():
        loads = [
            pltpu.make_async_copy(v_hbm, v_ref, sem.at[0]),
            pltpu.make_async_copy(t_hbm, t_ref, sem.at[1]),
        ]
        for load in loads:
            load.start()
        for load in loads:
            load.wait()
        count = v_ref.shape[0]
        _, _, diagonal, _ = form_system(v_ref[...], split_ref)
        rhs = wanted_rows(ids_ref, count)
        scale = 1.0 / diagonal

        def ratio(a, b):
            return jnp.where(b > 0.0, a / jnp.where(b > 0.0, b, 1.0), 0.0)

        def unfinished(state):
            step, _, _, _, rz = state
            return (step < MOST_STEPS) & (jnp.max(rz - goal) > 0.0)

        def advance(state):
            step, sol, res, p, rz = state
            q = times_system(p, split_ref)
            alpha = ratio(rz, inner(p, q))
            sol = sol + alpha * p
            res = res - alpha * q
            zed = res * scale
            new = inner(res, zed)
            p = zed + ratio(new, rz) * p
            return step + 1, sol, res, p, new

        zed = rhs * scale
        rz = inner(rhs, zed)
        goal = rz * 1e-12
        state = (jnp.int32(0), jnp.zeros_like(rhs), rhs, zed, rz)
        sol = lax.while_loop(unfinished, advance, state)[1]
        out_ref[...] = scores_of(sol, v_ref[...], t_ref[...])[0:2]


def body(
    clip_acts, clip_cotangents, weight_in, weight_out, proj_in, proj_out, test_grads, clip_ids
):
    width = proj_in.shape[1] * proj_out.shape[1]
    count = 2 * HALF
    full = jax.ShapeDtypeStruct((count, width), BF16)
    vmem = pl.BlockSpec(memory_space=pltpu.VMEM)
    smem = pl.BlockSpec(memory_space=pltpu.SMEM)
    hbm = pl.BlockSpec(memory_space=pl.ANY)
    dma = pltpu.SemaphoreType.DMA

    def like(array):
        return pltpu.VMEM(array.shape, array.dtype)

    raw, check, v_all, t_all = pl.pallas_call(
        main_kernel,
        out_shape=(
            jax.ShapeDtypeStruct((8, count), F32),
            jax.ShapeDtypeStruct((8, 128), F32),
            full,
            full,
        ),
        in_specs=[smem] + [hbm] * 6 + [vmem],
        out_specs=(vmem, vmem, hbm, hbm),
        scratch_shapes=[
            like(clip_acts),
            like(clip_cotangents),
            like(weight_in),
            like(weight_out),
            like(proj_in),
            like(proj_out),
            like(full),
            like(full),
            pltpu.VMEM((2, TILE, 128), BF16),
            pltpu.VMEM((2, NZ, TILE, 128), BF16),
            pltpu.VMEM((NZ * TILE, 128), F32),
            pltpu.VMEM((count, 3 * count), BF16),
            pltpu.VMEM((count, count), BF16),
            dma((4,)),
            dma((PARTS,)),
            dma((PARTS,)),
            dma((2,)),
            dma((2, NZ - 1)),
            dma((2, NZ - 1)),
            dma((2, STEPS)),
            dma((2, STEPS)),
            dma((2, STEPS + 1)),
            dma((2, STEPS + 1)),
        ],
        compiler_params=pltpu.CompilerParams(
            collective_id=0, has_side_effects=True, vmem_limit_bytes=56 << 20
        ),
    )(
        clip_ids,
        clip_acts,
        clip_cotangents,
        weight_in,
        weight_out,
        proj_in,
        proj_out,
        test_grads,
    )
    return pl.pallas_call(
        finish_kernel,
        out_shape=jax.ShapeDtypeStruct((2, count), F32),
        in_specs=[smem, vmem, vmem, hbm, hbm],
        out_specs=vmem,
        scratch_shapes=[
            like(full),
            like(full),
            pltpu.VMEM((count, 3 * count), BF16),
            dma((2,)),
        ],
        compiler_params=pltpu.CompilerParams(vmem_limit_bytes=56 << 20),
    )(clip_ids, raw, check, v_all, t_all)


def solution(mesh):
    in_specs = (
        P(("clip", "proj"), None, None),
        P(("clip", "proj"), None, None),
        P(),
        P(),
        P(),
        P(),
        P(("clip", "proj"), None),
        P(("clip", "proj")),
    )
    out_specs = P(("clip", "proj"), None)
    return jax.shard_map(body, mesh=mesh, in_specs=in_specs, out_specs=out_specs, check_vma=False)
```

time: 1570 us -> 75.8 us (0.05)
  waiting for transfers between devices: 1050 us -> 0 us
  other arithmetic: 261 us -> 0 us
  blocking collectives: 127 us -> 0 us
  Pallas kernels: 0 us -> 71.8 us
  matrix products: 57.8 us -> 0 us
  local copies, waits for them, and re-layouts: 44 us -> 3.74 us
  between operations: 19.7 us -> 0.01 us
    psum x1 -> x0, waiting for transfers between devices: 649 us -> none  [body(): slab_sum = lax.psum(slab_term, 'clip')]
    all_gather x2 -> x0, waiting for transfers between devices: 400 us -> none  [the longest x1 400 us: body(): all_tests = lax.all_gather(solved.T, ('clip', 'proj'), axis=0, tiled=True)]
    another operation x33 -> x0, other arithmetic: 251 us -> none  [the longest x30 167 us: body(): factor = jnp.linalg.cholesky(system)]
    psum x1 -> x0, blocking collectives: 121 us -> none  [body(): square_total = lax.psum(jnp.sum(widened * widened), ('clip', 'proj'))]
    pallas_call x0 -> x2, Pallas kernels: none -> 71.8 us  [the longest x1 40.6 us: body(): pl.pallas_call(main_kernel, out_shape=(jax.ShapeDtypeStruct((8, count), F...]
    another operation x44 -> x0, matrix products: 46.8 us -> none  [the longest x14 26.1 us: body(): factor = jnp.linalg.cholesky(system)]
    another operation x70 -> x0, local copies, waits for them, and re-layouts: 29.3 us -> none
  transfers between devices with their start and end apart: 3 -> 0, of which waited for: 2 -> 0; matrix products, arithmetic and copies ran while one was open for 0% -> 0% of each run, Pallas kernels for 0% -> 0%
where the time goes in v2:
time: 75.8 us; the launch traced here: 75.5 us
  Pallas kernels  71.8 us (95%)
  local copies, waits for them, and re-layouts  3.74 us (5%)
    pallas_call x1, Pallas kernels, body(): pl.pallas_call(main_kernel, out_shape=(jax.ShapeDtypeStruct((8, count), F...  40.6 us
    pallas_call x1, Pallas kernels, body(): pl.pallas_call(finish_kernel, out_shape=jax.ShapeDtypeStruct((2, count),...  31.2 us
    unnamed x2, local copies, waits for them, and re-layouts  3.74 us

profile of v2, /device:TPU:3, one launch (start us, length us, event | category | flops | bytes accessed | tf_op | source)
XLA Modules:
  0.0 75.5 jit_solution(845547418282995540)
XLA Ops:
  0.0 1.6 %copy.9.proj_in_hbm = bf16[768,32]{1,0:T(8,128)(2,1)} copy(bf16[768,32]{0,1:T(8,128)(2,1)} %param.12) | data formatting | bytes 98304 | tf_op args[4]
  1.6 2.1 %copy.10.proj_out_hbm = bf16[3072,32]{1,0:T(8,128)(2,1)} copy(bf16[3072,32]{0,1:T(8,128)(2,1)} %param.13) | data formatting | bytes 393216 | tf_op args[5]
  3.7 40.6 %shard_map.82 = (f32[8,512]{1,0:T(8,128)}, f32[8,128]{1,0:T(8,128)}, bf16[512,1024]{1,0:T(8,128)(2,1)}, bf16[512,1024]{1,0:T(8,128)(2,1)}) custom-call(s32[2]{0:T(128)} %ids_ref.3, bf16[2,64,768]{2,1,0:T(8,128)(2,1)} %acts_hbm.1, bf16[2,64,768]{2,1,0:T(8,128)(2,1)} %cot_hbm.1, bf16[768,3072]{1,0:T(8,128)(2,1)} %w_in_hbm.1, bf16[3072,768]{1,0:T(8,128)(2,1)} %w_out_hbm.1, ...), custom_call_target="tpu_custom_call" | custom-call | tf_op jit(solution)/shard_map/pallas_call | solution.py:437
  44.4 31.2 %shard_map.83 = f32[2,512]{1,0:T(2,128)} custom-call(s32[2]{0:T(128)} %ids_ref.3, f32[8,512]{1,0:T(8,128)} %get-tuple-element.9.raw_ref, f32[8,128]{1,0:T(8,128)} %get-tuple-element.10.check_ref, bf16[512,1024]{1,0:T(8,128)(2,1)} %get-tuple-element.11.v_hbm, bf16[512,1024]{1,0:T(8,128)(2,1)} %get-tuple-element.12.t_hbm), custom_call_target="tpu_custom_call" | custom-call | tf_op jit(solution)/shard_map/pallas_call | solution.py:485

commit v3 on v2

--- a/solution.py
+++ b/solution.py
@@ -17,7 +17,7 @@
 TILE = 16
 ROWS = 2 * NZ
 HALF = PLANE * ROWS
-PARTS = 6
+PARTS = 2
 DOUBLINGS = 4
 REFINEMENTS = 3
 MOST_STEPS = 4096
@@ -28,7 +28,6 @@
     key=lambda s: min(s[0], NY - s[0]) + min(s[1], NX - s[1]),
 )
 STEPS = len(PLANE_STEPS)
-BACK = [(NY - s[0], NX - s[1]) for s in PLANE_STEPS]
 
 
 def gelu_slope(values):
@@ -92,13 +91,13 @@
 
 
 def left_pieces(acts, proj_in):
-    tokens, width = acts.shape[0], proj_in.shape[1]
-    r, c = iota((width, 128), 0), iota((width, 128), 1)
+    tokens, width = acts.shape[0], proj_in.shape[0]
     groups = 128 // width
     per = width // groups
+    r, c = iota((128, width), 1), iota((128, width), 0)
     chosen = (c < width) & (r == lax.rem(c, per) * groups + c // per)
-    ordered = mm(proj_in, jnp.where(chosen, 1.0, 0.0).astype(BF16)).astype(BF16)
-    left = jnp.transpose(mm(acts, ordered))
+    ordered = mm(jnp.where(chosen, 1.0, 0.0).astype(BF16), proj_in).astype(BF16)
+    left = mm_t(ordered, acts)
     half = tokens // 2
     rows = []
     for k in range(2):
@@ -216,7 +215,7 @@
 ):
     y, x, z, core = my_place()
     other = 1 - core
-    chunks = v_all.shape[1] // 128
+    chunks = v_all.shape[-1] // 128
     block = w_in.shape[1] // PARTS
     tokens = acts.shape[0] * acts.shape[1]
 
@@ -258,79 +257,60 @@
     for target in targets:
         pl.semaphore_signal(barrier, inc=1, device_id=target, device_id_type=MESH)
 
-    def rows_of(place, of_core):
-        start = of_core * HALF + (place[0] * NX + place[1]) * ROWS
-        return pl.ds(pl.multiple_of(start, ROWS), ROWS)
-
-    def z_copy(a, d, slot):
+    fulls = (v_all, t_all)
+    mine = y * NX + x
+
+    def z_copy(a, d):
         return pltpu.make_async_remote_copy(
             src_ref=tiles.at[a],
-            dst_ref=line.at[a, slot],
-            send_sem=z_send.at[a, d - 1],
-            recv_sem=z_recv.at[a, d - 1],
+            dst_ref=line.at[a, z],
+            send_sem=z_send.at[a],
+            recv_sem=z_recv.at[a],
             device_id=targets[d - 1],
             device_id_type=MESH,
         )
 
-    fulls = (v_all, t_all)
-
-    def p_copy(a, k, place):
-        rows = fulls[a].at[rows_of(place, core)]
+    def p_copy(a, k):
+        step = PLANE_STEPS[k]
+        rows = fulls[a].at[core, mine]
+        group = step[0] if a == 0 else NY
         return pltpu.make_async_remote_copy(
             src_ref=rows,
             dst_ref=rows,
-            send_sem=p_send.at[a, k],
-            recv_sem=p_recv.at[a, k],
+            send_sem=p_send.at[a],
+            recv_sem=p_recv.at[group],
             device_id=targets[NZ - 1 + k],
             device_id_type=MESH,
         )
 
-    def c_copy(a, k, place, of_core):
-        rows = fulls[a].at[rows_of(place, of_core)]
+    def c_copy(i, src, dst):
         return pltpu.make_async_remote_copy(
-            src_ref=rows,
-            dst_ref=rows,
-            send_sem=c_send.at[a, k],
-            recv_sem=c_recv.at[a, k],
+            src_ref=src,
+            dst_ref=dst,
+            send_sem=c_send.at[i],
+            recv_sem=c_recv.at[i],
             device_id=targets[-1],
             device_id_type=MESH,
         )
 
+    def arrived(ref, sem):
+        pltpu.make_async_copy(ref, ref, sem).wait()
+
     def start_line(a, tile):
         tiles[a] = tile
         for d in range(1, NZ):
-            z_copy(a, d, z).start()
+            z_copy(a, d).start()
         line[a, z] = tile
 
     def start_plane(a):
-        for d in range(1, NZ):
-            z_copy(a, d, lax.rem(z + NZ - d, NZ)).wait_recv()
+        arrived(line.at[a, pl.ds(0, NZ - 1)], z_recv.at[a])
         wide[...] = line[a].reshape(NZ * TILE, 128).astype(F32)
-        mine = rows_of((y, x), core)
         for c in range(chunks):
-            fulls[a][mine, c * 128 : (c + 1) * 128] = wide[
+            fulls[a][core, mine, :, c * 128 : (c + 1) * 128] = wide[
                 pl.ds(c, ROWS, stride=chunks), :
             ].astype(BF16)
         for k in range(STEPS):
-            p_copy(a, k, (y, x)).start()
-        c_copy(a, 0, (y, x), core).start()
-
-    def forward(a):
-        for k, s in enumerate(BACK):
-            p_copy(a, k, in_plane(s)).wait_recv()
-            c_copy(a, k + 1, in_plane(s), core).start()
-
-    def finish(a):
-        for k, s in enumerate([(0, 0)] + BACK):
-            c_copy(a, k, in_plane(s), other).wait_recv()
-
-    def settle(a):
-        for d in range(1, NZ):
-            z_copy(a, d, z).wait_send()
-        for k in range(STEPS):
-            p_copy(a, k, (y, x)).wait_send()
-        for k, s in enumerate([(0, 0)] + BACK):
-            c_copy(a, k, in_plane(s), core).wait_send()
+            p_copy(a, k).start()
 
     t_tile = spread(wide.at[pl.ds(0, TILE)], t_ref[...].astype(F32))
     pl.semaphore_wait(barrier, len(targets))
@@ -349,27 +329,42 @@
         preact = mm(acts[...].reshape(tokens, -1), w_in[:, part])
         backprop = mm_t(cot[...].reshape(tokens, -1), w_out[part])
         deltas = (backprop * gelu_slope(preact)).astype(BF16)
-        term = mm(deltas, proj_out[part])
+        term = mm_t(deltas, proj_out[:, part])
         right = term if right is None else right + term
-        if i == 1:
+        if i == 0:
             start_plane(1)
-    outer = outer_tile(left, right, proj_in.shape[1])
+    outer = outer_tile(left, right, proj_in.shape[0])
     start_line(0, (outer * (1.0 / math.sqrt(acts.shape[1]))).astype(BF16))
-    forward(1)
     start_plane(0)
-    finish(1)
+
+    arrived(t_all.at[core, pl.ds(0, STEPS)], p_recv.at[NY])
+    t_copy = c_copy(NY, t_all.at[core], t_all.at[core])
+    t_copy.start()
+    v_copies = []
+    for i in range(NY):
+        first = lax.rem(y + NY - i, NY) * NX
+        arrived(v_all.at[core, pl.ds(first, NX - (i == 0))], p_recv.at[i])
+        rows = v_all.at[core, pl.ds(first, NX)]
+        v_copies.append(c_copy(i, rows, rows))
+        v_copies[-1].start()
+    t_copy.wait_recv()
     store_t = pltpu.make_async_copy(t_all, t_out, store_sem.at[1])
     store_t.start()
-    forward(0)
-    finish(0)
+    for copy in v_copies:
+        copy.wait_recv()
     store_v = pltpu.make_async_copy(v_all, v_out, store_sem.at[0])
     store_v.start()
 
-    sol, excess = refined(ids_ref, v_all[...], split_ref, m_ref)
-    raw_ref[...] = scores_of(sol, v_all[...], t_all[...])
+    v = v_all[...].reshape(2 * HALF, -1)
+    sol, excess = refined(ids_ref, v, split_ref, m_ref)
+    raw_ref[...] = scores_of(sol, v, t_all[...].reshape(2 * HALF, -1))
     check_ref[...] = jnp.broadcast_to(excess, check_ref.shape)
-    settle(1)
-    settle(0)
+    for a in range(2):
+        arrived(line.at[a, pl.ds(0, NZ - 1)], z_send.at[a])
+        arrived(fulls[a].at[core, pl.ds(0, STEPS)], p_send.at[a])
+    t_copy.wait_send()
+    for copy in v_copies:
+        copy.wait_send()
     store_t.wait()
     store_v.wait()
 
@@ -389,8 +384,9 @@
             load.start()
         for load in loads:
             load.wait()
-        count = v_ref.shape[0]
-        _, _, diagonal, _ = form_system(v_ref[...], split_ref)
+        count = 2 * HALF
+        v, t = v_ref[...].reshape(count, -1), t_ref[...].reshape(count, -1)
+        _, _, diagonal, _ = form_system(v, split_ref)
         rhs = wanted_rows(ids_ref, count)
         scale = 1.0 / diagonal
 
@@ -417,15 +413,16 @@
         goal = rz * 1e-12
         state = (jnp.int32(0), jnp.zeros_like(rhs), rhs, zed, rz)
         sol = lax.while_loop(unfinished, advance, state)[1]
-        out_ref[...] = scores_of(sol, v_ref[...], t_ref[...])[0:2]
+        out_ref[...] = scores_of(sol, v, t)[0:2]
 
 
 def body(
     clip_acts, clip_cotangents, weight_in, weight_out, proj_in, proj_out, test_grads, clip_ids
 ):
     width = proj_in.shape[1] * proj_out.shape[1]
+    proj_in, proj_out = proj_in.T, proj_out.T
     count = 2 * HALF
-    full = jax.ShapeDtypeStruct((count, width), BF16)
+    full = jax.ShapeDtypeStruct((2, PLANE, ROWS, width), BF16)
     vmem = pl.BlockSpec(memory_space=pltpu.VMEM)
     smem = pl.BlockSpec(memory_space=pltpu.SMEM)
     hbm = pl.BlockSpec(memory_space=pl.ANY)
@@ -462,12 +459,12 @@
             dma((PARTS,)),
             dma((PARTS,)),
             dma((2,)),
-            dma((2, NZ - 1)),
-            dma((2, NZ - 1)),
-            dma((2, STEPS)),
-            dma((2, STEPS)),
-            dma((2, STEPS + 1)),
-            dma((2, STEPS + 1)),
+            dma((2,)),
+            dma((2,)),
+            dma((2,)),
+            dma((NY + 1,)),
+            dma((NY + 1,)),
+            dma((NY + 1,)),
         ],
         compiler_params=pltpu.CompilerParams(
             collective_id=0, has_side_effects=True, vmem_limit_bytes=56 << 20

time: 75.8 us -> 70.8 us (0.934)
  local copies, waits for them, and re-layouts: 3.74 us -> 0 us
  Pallas kernels: 71.8 us -> 70.2 us
    unnamed x2 -> x0, local copies, waits for them, and re-layouts: 3.74 us -> none
    pallas_call x1, Pallas kernels: 40.6 us -> 38.5 us  [body(): pl.pallas_call(main_kernel, out_shape=(jax.ShapeDtypeStruct((8, count), F...]
where the time goes in v3:
time: 70.8 us; the launch traced here: 70.3 us
  Pallas kernels  70.2 us (99%)
    pallas_call x1, Pallas kernels, body(): pl.pallas_call(main_kernel, out_shape=(jax.ShapeDtypeStruct((8, count), F...  38.5 us
    pallas_call x1, Pallas kernels, body(): pl.pallas_call(finish_kernel, out_shape=jax.ShapeDtypeStruct((2, count),...  31.8 us

profile of v3, /device:TPU:3, one launch (start us, length us, event | category | flops | bytes accessed | tf_op | source)
XLA Modules:
  0.0 70.3 jit_solution(16698782001126974762)
XLA Ops:
  0.0 38.5 %shard_map.82 = (f32[8,512]{1,0:T(8,128)}, f32[8,128]{1,0:T(8,128)}, bf16[2,16,16,1024]{3,2,1,0:T(8,128)(2,1)}, bf16[2,16,16,1024]{3,2,1,0:T(8,128)(2,1)}) custom-call(s32[2]{0:T(128)} %ids_ref.3, bf16[2,64,768]{2,1,0:T(8,128)(2,1)} %acts_hbm.1, bf16[2,64,768]{2,1,0:T(8,128)(2,1)} %cot_hbm.1, bf16[768,3072]{1,0:T(8,128)(2,1)} %w_in_hbm.1, ...), custom_call_target="tpu_custom_call" | custom-call | tf_op jit(solution)/shard_map/pallas_call | solution.py:434
  38.5 31.8 %shard_map.83 = f32[2,512]{1,0:T(2,128)} custom-call(s32[2]{0:T(128)} %ids_ref.3, f32[8,512]{1,0:T(8,128)} %get-tuple-element.9.raw_ref, f32[8,128]{1,0:T(8,128)} %get-tuple-element.10.check_ref, bf16[2,16,16,1024]{3,2,1,0:T(8,128)(2,1)} %get-tuple-element.11.v_hbm, bf16[2,16,16,1024]{3,2,1,0:T(8,128)(2,1)} %get-tuple-element.12.t_hbm), custom_call_target="tpu_custom_call" | custom-call | tf_op jit(solution)/shard_map/pallas_call | solution.py:482

commit v4 on v3

--- a/solution.py
+++ b/solution.py
@@ -25,9 +25,13 @@
 
 PLANE_STEPS = sorted(
     ((dy, dx) for dy in range(NY) for dx in range(NX) if (dy, dx) != (0, 0)),
-    key=lambda s: min(s[0], NY - s[0]) + min(s[1], NX - s[1]),
+    key=lambda s: -(min(s[0], NY - s[0]) + min(s[1], NX - s[1])),
 )
 STEPS = len(PLANE_STEPS)
+LINE_STEPS = sorted(range(1, NZ), key=lambda d: -min(d, NZ - d))
+CHUNKS = 8
+ACROSS = 6
+SPLIT = ACROSS * 128
 
 
 def gelu_slope(values):
@@ -132,15 +136,15 @@
     x_lo, z = lax.rem(j // 4, XLO), lax.rem(j // (4 * XLO), NZ)
     rest = j // (4 * XLO * NZ)
     x_hi, y = lax.rem(rest, NX // XLO), rest // (NX // XLO)
-    source = core * HALF + (y * NX + x_hi * XLO + x_lo) * ROWS + z * 2 + k
+    source = core * HALF + (y * NX + x_hi * XLO + x_lo) * ROWS + k * NZ + z
     return jnp.where(iota(shape, 0) == source, 1.0, 0.0).astype(BF16)
 
 
 def wanted_rows(ids_ref, count):
     y, x, z, core = my_place()
-    base = core * HALF + (y * NX + x) * ROWS + z * 2
+    base = core * HALF + (y * NX + x) * ROWS + z
     lane, sub = iota((8, count), 1), iota((8, count), 0)
-    wanted = jnp.where(sub == 0, base + ids_ref[0], base + ids_ref[1])
+    wanted = base + NZ * jnp.where(sub == 0, ids_ref[0], ids_ref[1])
     return jnp.where((lane == wanted) & (sub < 2), 1.0, 0.0)
 
 
@@ -208,21 +212,29 @@
 
 
 def main_kernel(
-    ids_ref, acts_hbm, cot_hbm, w_in_hbm, w_out_hbm, proj_in_hbm, proj_out_hbm, t_ref,
+    ids_hbm, acts_hbm, cot_hbm, w_in_hbm, w_out_hbm, proj_in_hbm, proj_out_hbm, test_hbm,
     raw_ref, check_ref, v_out, t_out,
-    acts, cot, w_in, w_out, proj_in, proj_out, v_all, t_all, tiles, line, wide, split_ref, m_ref,
-    load_sem, in_sem, out_sem, store_sem, z_send, z_recv, p_send, p_recv, c_send, c_recv,
+    ids_ref, acts, cot, w_in, w_out, proj_in, proj_out, test, v_all, t_all,
+    tiles, line, plane, cross, wide, split_ref, m_ref,
+    load_sem, in_sem, out_sem, store_sem,
+    line_send, line_recv, plane_send, plane_recv,
+    rows_send, rows_recv, cross_send, cross_recv, core_send, core_recv,
 ):
     y, x, z, core = my_place()
-    other = 1 - core
-    chunks = v_all.shape[-1] // 128
     block = w_in.shape[1] // PARTS
     tokens = acts.shape[0] * acts.shape[1]
 
     small = [
         pltpu.make_async_copy(src, dst, load_sem.at[i])
         for i, (src, dst) in enumerate(
-            ((acts_hbm, acts), (proj_in_hbm, proj_in), (cot_hbm, cot), (proj_out_hbm, proj_out))
+            (
+                (acts_hbm, acts),
+                (proj_in_hbm, proj_in),
+                (cot_hbm, cot),
+                (proj_out_hbm, proj_out),
+                (test_hbm, test),
+                (ids_hbm, ids_ref),
+            )
         )
     ]
     loads_in, loads_out = [], []
@@ -234,6 +246,7 @@
         loads_out.append(
             pltpu.make_async_copy(w_out_hbm.at[part], w_out.at[part], out_sem.at[i])
         )
+    small[4].start()
     small[0].start()
     small[1].start()
     loads_in[0].start()
@@ -243,78 +256,90 @@
     for i in range(1, PARTS):
         loads_in[i].start()
         loads_out[i].start()
-
-    def along_z(d):
-        return lax.rem(z + d, NZ)
-
-    def in_plane(step):
-        return lax.rem(y + step[0], NY), lax.rem(x + step[1], NX)
+    small[5].start()
 
     barrier = pltpu.get_barrier_semaphore()
-    targets = [device_at(y, x, along_z(d), core) for d in range(1, NZ)]
-    targets += [device_at(*in_plane(s), z, core) for s in PLANE_STEPS]
-    targets += [device_at(y, x, z, other)]
+    on_line = [device_at(y, x, lax.rem(z + d, NZ), core) for d in LINE_STEPS]
+    on_plane = [
+        device_at(lax.rem(y + dy, NY), lax.rem(x + dx, NX), z, core) for dy, dx in PLANE_STEPS
+    ]
+    partner = device_at(y, x, z, 1 - core)
+    targets = on_line + on_plane + [partner]
     for target in targets:
         pl.semaphore_signal(barrier, inc=1, device_id=target, device_id_type=MESH)
 
     fulls = (v_all, t_all)
     mine = y * NX + x
 
-    def z_copy(a, d):
-        return pltpu.make_async_remote_copy(
-            src_ref=tiles.at[a],
-            dst_ref=line.at[a, z],
-            send_sem=z_send.at[a],
-            recv_sem=z_recv.at[a],
-            device_id=targets[d - 1],
+    def send(src, dst, send_sem, recv_sem, target):
+        pltpu.make_async_remote_copy(
+            src_ref=src,
+            dst_ref=dst,
+            send_sem=send_sem,
+            recv_sem=recv_sem,
+            device_id=target,
             device_id_type=MESH,
-        )
-
-    def p_copy(a, k):
-        step = PLANE_STEPS[k]
-        rows = fulls[a].at[core, mine]
-        group = step[0] if a == 0 else NY
+        ).start()
+
+    def await_bytes(ref, sem):
+        pltpu.make_async_copy(ref, ref, sem).wait()
+
+    def start_tiles(a, tile):
+        tiles[a] = tile
+        for target in on_line:
+            send(tiles.at[a], line.at[a, z], line_send.at[a], line_recv.at[a], target)
+        for target in on_plane:
+            send(tiles.at[a], plane.at[a, mine], plane_send.at[a], plane_recv.at[a], target)
+        line[a, z] = tile
+        plane[a, mine] = tile
+
+    def start_blocks(a):
+        full = fulls[a]
+        await_bytes(line.at[a, pl.ds(0, NZ - 1)], line_recv.at[a])
+        wide[0 : NZ * TILE, :] = line[a].reshape(NZ * TILE, 128).astype(F32)
+        for c in range(ACROSS):
+            both = [wide[pl.ds(k * CHUNKS + c, NZ, stride=TILE), :] for k in range(2)]
+            full[core, mine, :, c * 128 : (c + 1) * 128] = jnp.concatenate(both, axis=0).astype(
+                BF16
+            )
+        rows = full.at[core, mine, :, pl.ds(0, SPLIT)]
+        for (dy, _), target in zip(PLANE_STEPS, on_plane):
+            send(rows, rows, rows_send.at[a], rows_recv.at[dy if a == 0 else NY], target)
+        await_bytes(plane.at[a, pl.ds(0, STEPS)], plane_recv.at[a])
+        wide[...] = plane[a].reshape(PLANE * TILE, 128).astype(F32)
+        for c in range(ACROSS, CHUNKS):
+            both = [wide[pl.ds(k * CHUNKS + c, PLANE, stride=TILE), :] for k in range(2)]
+            cross[a, z, :, (c - ACROSS) * 128 : (c - ACROSS + 1) * 128] = jnp.concatenate(
+                both, axis=0
+            ).astype(BF16)
+        rows = cross.at[a, z]
+        for target in on_line:
+            send(rows, rows, cross_send.at[a], cross_recv.at[a], target)
+
+    def place_cross(a):
+        await_bytes(cross.at[a, pl.ds(0, NZ - 1)], cross_recv.at[a])
+        for c in range(CHUNKS - ACROSS):
+            wide[...] = cross[a, :, :, c * 128 : (c + 1) * 128].reshape(NZ * 2 * PLANE, 128).astype(F32)
+            for p in range(PLANE):
+                both = [wide[pl.ds(k * PLANE + p, NZ, stride=2 * PLANE), :] for k in range(2)]
+                fulls[a][core, p, :, SPLIT + c * 128 : SPLIT + (c + 1) * 128] = jnp.concatenate(
+                    both, axis=0
+                ).astype(BF16)
+
+    def core_copy(i, rows):
         return pltpu.make_async_remote_copy(
             src_ref=rows,
             dst_ref=rows,
-            send_sem=p_send.at[a],
-            recv_sem=p_recv.at[group],
-            device_id=targets[NZ - 1 + k],
+            send_sem=core_send.at[i],
+            recv_sem=core_recv.at[i],
+            device_id=partner,
             device_id_type=MESH,
         )
 
-    def c_copy(i, src, dst):
-        return pltpu.make_async_remote_copy(
-            src_ref=src,
-            dst_ref=dst,
-            send_sem=c_send.at[i],
-            recv_sem=c_recv.at[i],
-            device_id=targets[-1],
-            device_id_type=MESH,
-        )
-
-    def arrived(ref, sem):
-        pltpu.make_async_copy(ref, ref, sem).wait()
-
-    def start_line(a, tile):
-        tiles[a] = tile
-        for d in range(1, NZ):
-            z_copy(a, d).start()
-        line[a, z] = tile
-
-    def start_plane(a):
-        arrived(line.at[a, pl.ds(0, NZ - 1)], z_recv.at[a])
-        wide[...] = line[a].reshape(NZ * TILE, 128).astype(F32)
-        for c in range(chunks):
-            fulls[a][core, mine, :, c * 128 : (c + 1) * 128] = wide[
-                pl.ds(c, ROWS, stride=chunks), :
-            ].astype(BF16)
-        for k in range(STEPS):
-            p_copy(a, k).start()
-
-    t_tile = spread(wide.at[pl.ds(0, TILE)], t_ref[...].astype(F32))
+    small[4].wait()
+    t_tile = spread(wide.at[pl.ds(0, TILE)], test[...].astype(F32))
     pl.semaphore_wait(barrier, len(targets))
-    start_line(1, t_tile)
+    start_tiles(1, t_tile)
 
     small[0].wait()
     small[1].wait()
@@ -331,42 +356,46 @@
         deltas = (backprop * gelu_slope(preact)).astype(BF16)
         term = mm_t(deltas, proj_out[:, part])
         right = term if right is None else right + term
-        if i == 0:
-            start_plane(1)
     outer = outer_tile(left, right, proj_in.shape[0])
-    start_line(0, (outer * (1.0 / math.sqrt(acts.shape[1]))).astype(BF16))
-    start_plane(0)
-
-    arrived(t_all.at[core, pl.ds(0, STEPS)], p_recv.at[NY])
-    t_copy = c_copy(NY, t_all.at[core], t_all.at[core])
+    start_tiles(0, (outer * (1.0 / math.sqrt(acts.shape[1]))).astype(BF16))
+    start_blocks(1)
+    start_blocks(0)
+
+    place_cross(0)
+    v_copies = []
+    for dy in (0, 1, 3, 2):
+        first = lax.rem(y + NY - dy, NY) * NX
+        count = NX - (dy == 0)
+        await_bytes(v_all.at[core, pl.ds(first, count), :, pl.ds(0, SPLIT)], rows_recv.at[dy])
+        v_copies.append(core_copy(dy, v_all.at[core, pl.ds(first, NX)]))
+        v_copies[-1].start()
+    place_cross(1)
+    await_bytes(t_all.at[core, pl.ds(0, STEPS), :, pl.ds(0, SPLIT)], rows_recv.at[NY])
+    t_copy = core_copy(NY, t_all.at[core])
     t_copy.start()
-    v_copies = []
-    for i in range(NY):
-        first = lax.rem(y + NY - i, NY) * NX
-        arrived(v_all.at[core, pl.ds(first, NX - (i == 0))], p_recv.at[i])
-        rows = v_all.at[core, pl.ds(first, NX)]
-        v_copies.append(c_copy(i, rows, rows))
-        v_copies[-1].start()
-    t_copy.wait_recv()
-    store_t = pltpu.make_async_copy(t_all, t_out, store_sem.at[1])
-    store_t.start()
     for copy in v_copies:
         copy.wait_recv()
     store_v = pltpu.make_async_copy(v_all, v_out, store_sem.at[0])
     store_v.start()
 
+    small[5].wait()
     v = v_all[...].reshape(2 * HALF, -1)
     sol, excess = refined(ids_ref, v, split_ref, m_ref)
+    t_copy.wait_recv()
+    store_t = pltpu.make_async_copy(t_all, t_out, store_sem.at[1])
+    store_t.start()
     raw_ref[...] = scores_of(sol, v, t_all[...].reshape(2 * HALF, -1))
     check_ref[...] = jnp.broadcast_to(excess, check_ref.shape)
     for a in range(2):
-        arrived(line.at[a, pl.ds(0, NZ - 1)], z_send.at[a])
-        arrived(fulls[a].at[core, pl.ds(0, STEPS)], p_send.at[a])
+        await_bytes(line.at[a, pl.ds(0, NZ - 1)], line_send.at[a])
+        await_bytes(plane.at[a, pl.ds(0, STEPS)], plane_send.at[a])
+        await_bytes(fulls[a].at[core, pl.ds(0, STEPS), :, pl.ds(0, SPLIT)], rows_send.at[a])
+        await_bytes(cross.at[a, pl.ds(0, NZ - 1)], cross_send.at[a])
     t_copy.wait_send()
     for copy in v_copies:
         copy.wait_send()
+    store_v.wait()
     store_t.wait()
-    store_v.wait()
 
 
 def finish_kernel(ids_ref, raw_ref, check_ref, v_hbm, t_hbm, out_ref, v_ref, t_ref, split_ref, sem):
@@ -439,30 +468,38 @@
             full,
             full,
         ),
-        in_specs=[smem] + [hbm] * 6 + [vmem],
+        in_specs=[hbm] * 8,
         out_specs=(vmem, vmem, hbm, hbm),
         scratch_shapes=[
+            pltpu.SMEM(clip_ids.shape, clip_ids.dtype),
             like(clip_acts),
             like(clip_cotangents),
             like(weight_in),
             like(weight_out),
             like(proj_in),
             like(proj_out),
+            like(test_grads),
             like(full),
             like(full),
             pltpu.VMEM((2, TILE, 128), BF16),
             pltpu.VMEM((2, NZ, TILE, 128), BF16),
-            pltpu.VMEM((NZ * TILE, 128), F32),
+            pltpu.VMEM((2, PLANE, TILE, 128), BF16),
+            pltpu.VMEM((2, NZ, 2 * PLANE, (CHUNKS - ACROSS) * 128), BF16),
+            pltpu.VMEM((PLANE * TILE, 128), F32),
             pltpu.VMEM((count, 3 * count), BF16),
             pltpu.VMEM((count, count), BF16),
-            dma((4,)),
+            dma((6,)),
             dma((PARTS,)),
             dma((PARTS,)),
             dma((2,)),
             dma((2,)),
             dma((2,)),
             dma((2,)),
+            dma((2,)),
+            dma((2,)),
             dma((NY + 1,)),
+            dma((2,)),
+            dma((2,)),
             dma((NY + 1,)),
             dma((NY + 1,)),
         ],

time: 70.8 us -> 68.2 us (0.963)
  Pallas kernels: 70.2 us -> 67.6 us
    pallas_call x1, Pallas kernels: 38.5 us -> 34.6 us  [body(): pl.pallas_call(main_kernel, out_shape=(jax.ShapeDtypeStruct((8, count), F...]
    pallas_call x1, Pallas kernels: 31.8 us -> 33 us  [body(): pl.pallas_call(finish_kernel, out_shape=jax.ShapeDtypeStruct((2, count),...]
where the time goes in v4:
time: 68.2 us; the launch traced here: 67.6 us
  Pallas kernels  67.6 us (99%)
    pallas_call x1, Pallas kernels, body(): pl.pallas_call(main_kernel, out_shape=(jax.ShapeDtypeStruct((8, count), F...  34.6 us
    pallas_call x1, Pallas kernels, body(): pl.pallas_call(finish_kernel, out_shape=jax.ShapeDtypeStruct((2, count),...  33 us

profile of v4, /device:TPU:3, one launch (start us, length us, event | category | flops | bytes accessed | tf_op | source)
XLA Modules:
  0.0 67.6 jit_solution(13696071162819681141)
XLA Ops:
  0.0 34.6 %shard_map.82 = (f32[8,512]{1,0:T(8,128)}, f32[8,128]{1,0:T(8,128)}, bf16[2,16,16,1024]{3,2,1,0:T(8,128)(2,1)}, bf16[2,16,16,1024]{3,2,1,0:T(8,128)(2,1)}) custom-call(s32[2]{0:T(128)} %ids_ref.1, bf16[2,64,768]{2,1,0:T(8,128)(2,1)} %acts_hbm.1, bf16[2,64,768]{2,1,0:T(8,128)(2,1)} %cot_hbm.1, bf16[768,3072]{1,0:T(8,128)(2,1)} %w_in_hbm.1, ...), custom_call_target="tpu_custom_call" | custom-call | tf_op jit(solution)/shard_map/pallas_call | solution.py:463
  34.6 33.0 %shard_map.83 = f32[2,512]{1,0:T(2,128)} custom-call(s32[2]{0:T(128)} %ids_ref.1, f32[8,512]{1,0:T(8,128)} %get-tuple-element.9.raw_ref, f32[8,128]{1,0:T(8,128)} %get-tuple-element.10.check_ref, bf16[2,16,16,1024]{3,2,1,0:T(8,128)(2,1)} %get-tuple-element.11.v_hbm, bf16[2,16,16,1024]{3,2,1,0:T(8,128)(2,1)} %get-tuple-element.12.t_hbm), custom_call_target="tpu_custom_call" | custom-call | tf_op jit(solution)/shard_map/pallas_call | solution.py:519

commit v5 on v4

--- a/solution.py
+++ b/solution.py
@@ -174,7 +174,7 @@
     return unstacked(mm(stacked(raw), target_order((t.shape[0], t.shape[0]))))
 
 
-def refined(ids_ref, v, split_ref, m_ref):
+def approximate_inverse(v, split_ref, m_ref):
     count = v.shape[0]
     system, low, _, eye = form_system(v, split_ref)
     high = split_ref[:, 0:count]
@@ -196,9 +196,10 @@
             am = mm(high, rounded)
         m = c * (2.0 * m - mm(rounded, am.astype(BF16)))
     m_ref[...] = m.astype(BF16)
-
-    rhs = wanted_rows(ids_ref, count)
-
+    return top
+
+
+def refined(rhs, top, split_ref, m_ref):
     def precondition(r):
         return mm(jnp.concatenate([r, jnp.zeros_like(r)], axis=0).astype(BF16), m_ref[...])[0:8]
 
@@ -213,10 +214,10 @@
 
 def main_kernel(
     ids_hbm, acts_hbm, cot_hbm, w_in_hbm, w_out_hbm, proj_in_hbm, proj_out_hbm, test_hbm,
-    raw_ref, check_ref, v_out, t_out,
-    ids_ref, acts, cot, w_in, w_out, proj_in, proj_out, test, v_all, t_all,
+    raw_ref, check_ref, v_all, t_all,
+    ids_ref, acts, cot, w_in, w_out, proj_in, proj_out, test,
     tiles, line, plane, cross, wide, split_ref, m_ref,
-    load_sem, in_sem, out_sem, store_sem,
+    load_sem, in_sem, out_sem,
     line_send, line_recv, plane_send, plane_recv,
     rows_send, rows_recv, cross_send, cross_recv, core_send, core_recv,
 ):
@@ -358,32 +359,34 @@
         right = term if right is None else right + term
     outer = outer_tile(left, right, proj_in.shape[0])
     start_tiles(0, (outer * (1.0 / math.sqrt(acts.shape[1]))).astype(BF16))
+    start_blocks(0)
     start_blocks(1)
-    start_blocks(0)
-
-    place_cross(0)
-    v_copies = []
+
+    copies = []
+
+    def forward(i, rows):
+        copies.append(core_copy(i, rows))
+        copies[-1].start()
+
     for dy in (0, 1, 3, 2):
+        if dy == 2:
+            place_cross(0)
+            forward(0, v_all.at[core, :, :, pl.ds(SPLIT, (CHUNKS - ACROSS) * 128)])
         first = lax.rem(y + NY - dy, NY) * NX
         count = NX - (dy == 0)
         await_bytes(v_all.at[core, pl.ds(first, count), :, pl.ds(0, SPLIT)], rows_recv.at[dy])
-        v_copies.append(core_copy(dy, v_all.at[core, pl.ds(first, NX)]))
-        v_copies[-1].start()
+        forward(dy + 1, v_all.at[core, pl.ds(first, NX), :, pl.ds(0, SPLIT)])
+    for copy in copies:
+        copy.wait_recv()
+
+    small[5].wait()
+    v = v_all[...].reshape(2 * HALF, -1)
+    top = approximate_inverse(v, split_ref, m_ref)
     place_cross(1)
     await_bytes(t_all.at[core, pl.ds(0, STEPS), :, pl.ds(0, SPLIT)], rows_recv.at[NY])
-    t_copy = core_copy(NY, t_all.at[core])
-    t_copy.start()
-    for copy in v_copies:
-        copy.wait_recv()
-    store_v = pltpu.make_async_copy(v_all, v_out, store_sem.at[0])
-    store_v.start()
-
-    small[5].wait()
-    v = v_all[...].reshape(2 * HALF, -1)
-    sol, excess = refined(ids_ref, v, split_ref, m_ref)
-    t_copy.wait_recv()
-    store_t = pltpu.make_async_copy(t_all, t_out, store_sem.at[1])
-    store_t.start()
+    forward(NY + 1, t_all.at[core])
+    sol, excess = refined(wanted_rows(ids_ref, 2 * HALF), top, split_ref, m_ref)
+    copies[-1].wait_recv()
     raw_ref[...] = scores_of(sol, v, t_all[...].reshape(2 * HALF, -1))
     check_ref[...] = jnp.broadcast_to(excess, check_ref.shape)
     for a in range(2):
@@ -391,28 +394,17 @@
         await_bytes(plane.at[a, pl.ds(0, STEPS)], plane_send.at[a])
         await_bytes(fulls[a].at[core, pl.ds(0, STEPS), :, pl.ds(0, SPLIT)], rows_send.at[a])
         await_bytes(cross.at[a, pl.ds(0, NZ - 1)], cross_send.at[a])
-    t_copy.wait_send()
-    for copy in v_copies:
+    for copy in copies:
         copy.wait_send()
-    store_v.wait()
-    store_t.wait()
-
-
-def finish_kernel(ids_ref, raw_ref, check_ref, v_hbm, t_hbm, out_ref, v_ref, t_ref, split_ref, sem):
+
+
+def finish_kernel(ids_ref, raw_ref, check_ref, v_ref, t_ref, out_ref, split_ref):
     out_ref[...] = raw_ref[0:2]
     excess = check_ref[...]
     fine = jnp.min(jnp.where(excess <= 0.0, 1.0, 0.0))
 
     @pl.when(fine < 1.0)
     def _():
-        loads = [
-            pltpu.make_async_copy(v_hbm, v_ref, sem.at[0]),
-            pltpu.make_async_copy(t_hbm, t_ref, sem.at[1]),
-        ]
-        for load in loads:
-            load.start()
-        for load in loads:
-            load.wait()
         count = 2 * HALF
         v, t = v_ref[...].reshape(count, -1), t_ref[...].reshape(count, -1)
         _, _, diagonal, _ = form_system(v, split_ref)
@@ -463,13 +455,13 @@
     raw, check, v_all, t_all = pl.pallas_call(
         main_kernel,
         out_shape=(
-            jax.ShapeDtypeStruct((8, count), F32),
-            jax.ShapeDtypeStruct((8, 128), F32),
-            full,
-            full,
+            pltpu.VMEM((8, count), F32),
+            pltpu.VMEM((8, 128), F32),
+            pltpu.VMEM(full.shape, BF16),
+            pltpu.VMEM(full.shape, BF16),
         ),
         in_specs=[hbm] * 8,
-        out_specs=(vmem, vmem, hbm, hbm),
+        out_specs=(vmem, vmem, vmem, vmem),
         scratch_shapes=[
             pltpu.SMEM(clip_ids.shape, clip_ids.dtype),
             like(clip_acts),
@@ -479,8 +471,6 @@
             like(proj_in),
             like(proj_out),
             like(test_grads),
-            like(full),
-            like(full),
             pltpu.VMEM((2, TILE, 128), BF16),
             pltpu.VMEM((2, NZ, TILE, 128), BF16),
             pltpu.VMEM((2, PLANE, TILE, 128), BF16),
@@ -496,12 +486,11 @@
             dma((2,)),
             dma((2,)),
             dma((2,)),
-            dma((2,)),
             dma((NY + 1,)),
             dma((2,)),
             dma((2,)),
-            dma((NY + 1,)),
-            dma((NY + 1,)),
+            dma((NY + 2,)),
+            dma((NY + 2,)),
         ],
         compiler_params=pltpu.CompilerParams(
             collective_id=0, has_side_effects=True, vmem_limit_bytes=56 << 20
@@ -519,16 +508,13 @@
     return pl.pallas_call(
         finish_kernel,
         out_shape=jax.ShapeDtypeStruct((2, count), F32),
-        in_specs=[smem, vmem, vmem, hbm, hbm],
+        in_specs=[smem, vmem, vmem, vmem, vmem],
         out_specs=vmem,
         scratch_shapes=[
-            like(full),
-            like(full),
             pltpu.VMEM((count, 3 * count), BF16),
-            dma((2,)),
         ],
-        compiler_params=pltpu.CompilerParams(vmem_limit_bytes=56 << 20),
-    )(clip_ids, raw, check, v_all, t_all)
+        compiler_params=pltpu.CompilerParams(vmem_limit_bytes=32 << 20),
+    )(clip_ids, *[pltpu.with_memory_space_constraint(r, pltpu.VMEM) for r in (raw, check, v_all, t_all)])
 
 
 def solution(mesh):

time: 68.2 us -> 62.4 us (0.915)
  the two profiles are of different devices: /device:TPU:3 before, /device:TPU:25 now
where the time goes in v5:
time: 62.4 us; the launch traced here: 62.3 us
  Pallas kernels  62.3 us (100%)
    pallas_call x1, Pallas kernels, body(): pl.pallas_call(main_kernel, out_shape=(pltpu.VMEM((8, count), F32), pltpu...  34.6 us
    pallas_call x1, Pallas kernels, body(): pl.pallas_call(finish_kernel, out_shape=jax.ShapeDtypeStruct((2, count),...  27.7 us

profile of v5, /device:TPU:25, one launch (start us, length us, event | category | flops | bytes accessed | tf_op | source)
XLA Modules:
  0.0 62.3 jit_solution(2655061985001057647)
XLA Ops:
  0.0 0.0 copy-start
  0.0 34.6 %shard_map.82 = (f32[8,512]{1,0:T(8,128)S(1)}, f32[8,128]{1,0:T(8,128)S(1)}, bf16[2,16,16,1024]{3,2,1,0:T(8,128)(2,1)S(1)}, bf16[2,16,16,1024]{3,2,1,0:T(8,128)(2,1)S(1)}) custom-call(s32[2]{0:T(128)} %ids_ref.1, bf16[2,64,768]{2,1,0:T(8,128)(2,1)} %acts_hbm.1, bf16[2,64,768]{2,1,0:T(8,128)(2,1)} %cot_hbm.1, bf16[768,3072]{1,0:T(8,128)(2,1)} %w_in_hbm.1, ...), custom_call_target="tpu_custom_call" | custom-call | tf_op jit(solution)/shard_map/pallas_call | solution.py:455
  34.6 0.0 copy-done
  34.6 27.7 %shard_map.83 = f32[2,512]{1,0:T(2,128)} custom-call(s32[2]{0:T(128)S(1)} %copy-done, f32[8,512]{1,0:T(8,128)S(1)} %get-tuple-element.9.raw_ref, f32[8,128]{1,0:T(8,128)S(1)} %get-tuple-element.10.check_ref, bf16[2,16,16,1024]{3,2,1,0:T(8,128)(2,1)S(1)} %get-tuple-element.11.v_ref, bf16[2,16,16,1024]{3,2,1,0:T(8,128)(2,1)S(1)} %get-tuple-element.12.t_ref), custom_call_target="tpu_custom_call" | custom-call | tf_op jit(solution)/shard_map/pallas_call | solution.py:508
Async XLA Ops:
  0.0 34.6 %copy-start = (s32[2]{0:T(128)S(1)}, s32[2]{0:T(128)}, u32[]{:S(2)}) copy-start(s32[2]{0:T(128)} %ids_ref.1) | copy-start | bytes 28

commit v6 on v5

--- a/solution.py
+++ b/solution.py
@@ -30,6 +30,7 @@
 STEPS = len(PLANE_STEPS)
 LINE_STEPS = sorted(range(1, NZ), key=lambda d: -min(d, NZ - d))
 CHUNKS = 8
+BEFORE, NEAR = 2, 5
 ACROSS = 6
 SPLIT = ACROSS * 128
 
@@ -141,8 +142,8 @@
 
 
 def wanted_rows(ids_ref, count):
-    y, x, z, core = my_place()
-    base = core * HALF + (y * NX + x) * ROWS + z
+    y, x, _, core = my_place()
+    base = core * HALF + (y * NX + x) * ROWS + BEFORE
     lane, sub = iota((8, count), 1), iota((8, count), 0)
     wanted = base + NZ * jnp.where(sub == 0, ids_ref[0], ids_ref[1])
     return jnp.where((lane == wanted) & (sub < 2), 1.0, 0.0)
@@ -216,10 +217,10 @@
     ids_hbm, acts_hbm, cot_hbm, w_in_hbm, w_out_hbm, proj_in_hbm, proj_out_hbm, test_hbm,
     raw_ref, check_ref, v_all, t_all,
     ids_ref, acts, cot, w_in, w_out, proj_in, proj_out, test,
-    tiles, line, plane, cross, wide, split_ref, m_ref,
+    tiles, t_tile, line, plane, cross, wide, split_ref, m_ref,
     load_sem, in_sem, out_sem,
-    line_send, line_recv, plane_send, plane_recv,
-    rows_send, rows_recv, cross_send, cross_recv, core_send, core_recv,
+    line_send, line_recv, plane_send, plane_recv, rows_send, rows_recv, cross_send, cross_recv,
+    v_send, v_recv, core_send, core_recv,
 ):
     y, x, z, core = my_place()
     block = w_in.shape[1] // PARTS
@@ -269,7 +270,6 @@
     for target in targets:
         pl.semaphore_signal(barrier, inc=1, device_id=target, device_id_type=MESH)
 
-    fulls = (v_all, t_all)
     mine = y * NX + x
 
     def send(src, dst, send_sem, recv_sem, target):
@@ -285,50 +285,8 @@
     def await_bytes(ref, sem):
         pltpu.make_async_copy(ref, ref, sem).wait()
 
-    def start_tiles(a, tile):
-        tiles[a] = tile
-        for target in on_line:
-            send(tiles.at[a], line.at[a, z], line_send.at[a], line_recv.at[a], target)
-        for target in on_plane:
-            send(tiles.at[a], plane.at[a, mine], plane_send.at[a], plane_recv.at[a], target)
-        line[a, z] = tile
-        plane[a, mine] = tile
-
-    def start_blocks(a):
-        full = fulls[a]
-        await_bytes(line.at[a, pl.ds(0, NZ - 1)], line_recv.at[a])
-        wide[0 : NZ * TILE, :] = line[a].reshape(NZ * TILE, 128).astype(F32)
-        for c in range(ACROSS):
-            both = [wide[pl.ds(k * CHUNKS + c, NZ, stride=TILE), :] for k in range(2)]
-            full[core, mine, :, c * 128 : (c + 1) * 128] = jnp.concatenate(both, axis=0).astype(
-                BF16
-            )
-        rows = full.at[core, mine, :, pl.ds(0, SPLIT)]
-        for (dy, _), target in zip(PLANE_STEPS, on_plane):
-            send(rows, rows, rows_send.at[a], rows_recv.at[dy if a == 0 else NY], target)
-        await_bytes(plane.at[a, pl.ds(0, STEPS)], plane_recv.at[a])
-        wide[...] = plane[a].reshape(PLANE * TILE, 128).astype(F32)
-        for c in range(ACROSS, CHUNKS):
-            both = [wide[pl.ds(k * CHUNKS + c, PLANE, stride=TILE), :] for k in range(2)]
-            cross[a, z, :, (c - ACROSS) * 128 : (c - ACROSS + 1) * 128] = jnp.concatenate(
-                both, axis=0
-            ).astype(BF16)
-        rows = cross.at[a, z]
-        for target in on_line:
-            send(rows, rows, cross_send.at[a], cross_recv.at[a], target)
-
-    def place_cross(a):
-        await_bytes(cross.at[a, pl.ds(0, NZ - 1)], cross_recv.at[a])
-        for c in range(CHUNKS - ACROSS):
-            wide[...] = cross[a, :, :, c * 128 : (c + 1) * 128].reshape(NZ * 2 * PLANE, 128).astype(F32)
-            for p in range(PLANE):
-                both = [wide[pl.ds(k * PLANE + p, NZ, stride=2 * PLANE), :] for k in range(2)]
-                fulls[a][core, p, :, SPLIT + c * 128 : SPLIT + (c + 1) * 128] = jnp.concatenate(
-                    both, axis=0
-                ).astype(BF16)
-
     def core_copy(i, rows):
-        return pltpu.make_async_remote_copy(
+        copy = pltpu.make_async_remote_copy(
             src_ref=rows,
             dst_ref=rows,
             send_sem=core_send.at[i],
@@ -336,11 +294,86 @@
             device_id=partner,
             device_id_type=MESH,
         )
+        copy.start()
+        return copy
+
+    def start_test_tiles(tile):
+        t_tile[...] = tile
+        for target in on_line:
+            send(t_tile, line.at[z], line_send, line_recv, target)
+        for target in on_plane:
+            send(t_tile, plane.at[mine], plane_send, plane_recv, target)
+        line[z] = tile
+        plane[mine] = tile
+
+    def start_test_blocks():
+        await_bytes(line.at[pl.ds(0, NZ - 1)], line_recv)
+        wide[0 : NZ * TILE, :] = line[...].reshape(NZ * TILE, 128).astype(F32)
+        for c in range(ACROSS):
+            both = [wide[pl.ds(k * CHUNKS + c, NZ, stride=TILE), :] for k in range(2)]
+            t_all[core, mine, :, c * 128 : (c + 1) * 128] = jnp.concatenate(both, axis=0).astype(
+                BF16
+            )
+        rows = t_all.at[core, mine, :, pl.ds(0, SPLIT)]
+        for target in on_plane:
+            send(rows, rows, rows_send, rows_recv, target)
+        await_bytes(plane.at[pl.ds(0, STEPS)], plane_recv)
+        wide[0 : PLANE * TILE, :] = plane[...].reshape(PLANE * TILE, 128).astype(F32)
+        for c in range(ACROSS, CHUNKS):
+            both = [wide[pl.ds(k * CHUNKS + c, PLANE, stride=TILE), :] for k in range(2)]
+            cross[z, :, (c - ACROSS) * 128 : (c - ACROSS + 1) * 128] = jnp.concatenate(
+                both, axis=0
+            ).astype(BF16)
+        rows = cross.at[z]
+        for target in on_line:
+            send(rows, rows, cross_send, cross_recv, target)
+
+    def place_test_blocks():
+        await_bytes(cross.at[pl.ds(0, NZ - 1)], cross_recv)
+        for c in range(CHUNKS - ACROSS):
+            columns = cross[:, :, c * 128 : (c + 1) * 128]
+            wide[0 : NZ * 2 * PLANE, :] = columns.reshape(NZ * 2 * PLANE, 128).astype(F32)
+            for p in range(PLANE):
+                both = [wide[pl.ds(k * PLANE + p, NZ, stride=2 * PLANE), :] for k in range(2)]
+                t_all[core, p, :, SPLIT + c * 128 : SPLIT + (c + 1) * 128] = jnp.concatenate(
+                    both, axis=0
+                ).astype(BF16)
+        await_bytes(t_all.at[core, pl.ds(0, STEPS), :, pl.ds(0, SPLIT)], rows_recv)
+
+    def start_vector_tiles(tile):
+        tiles[core, mine, BEFORE] = tile
+        own = tiles.at[core, mine, BEFORE]
+        for d, target in zip(LINE_STEPS, on_line):
+            slot = (BEFORE - d) % NZ
+            send(own, tiles.at[core, mine, slot], v_send.at[0], v_recv.at[int(slot >= NEAR)], target)
+
+    def pass_vector_tiles(far):
+        slots = pl.ds(NEAR, NZ - NEAR) if far else pl.ds(0, NEAR)
+        landed = pl.ds(0, NZ - NEAR if far else NEAR - 1)
+        await_bytes(tiles.at[core, mine, landed], v_recv.at[far])
+        rows = tiles.at[core, mine, slots]
+        for (dy, _), target in zip(PLANE_STEPS, on_plane):
+            send(rows, rows, v_send.at[1], v_recv.at[2 + dy], target)
+
+    def group_start(dy):
+        return lax.rem(y + NY - dy, NY) * NX
+
+    def lay_out(of_core, dy):
+        first = group_start(dy)
+        group = tiles[of_core, pl.ds(first, NX)]
+        wide[...] = group.reshape(NX * NZ * TILE, 128).astype(F32)
+        for p in range(NX):
+            for c in range(CHUNKS):
+                start = p * NZ * TILE + c
+                both = [wide[pl.ds(start + k * CHUNKS, NZ, stride=TILE), :] for k in range(2)]
+                v_all[of_core, first + p, :, c * 128 : (c + 1) * 128] = jnp.concatenate(
+                    both, axis=0
+                ).astype(BF16)
 
     small[4].wait()
-    t_tile = spread(wide.at[pl.ds(0, TILE)], test[...].astype(F32))
+    own_test = spread(wide.at[pl.ds(0, TILE)], test[...].astype(F32))
     pl.semaphore_wait(barrier, len(targets))
-    start_tiles(1, t_tile)
+    start_test_tiles(own_test)
 
     small[0].wait()
     small[1].wait()
@@ -358,42 +391,41 @@
         term = mm_t(deltas, proj_out[:, part])
         right = term if right is None else right + term
     outer = outer_tile(left, right, proj_in.shape[0])
-    start_tiles(0, (outer * (1.0 / math.sqrt(acts.shape[1]))).astype(BF16))
-    start_blocks(0)
-    start_blocks(1)
-
+    start_vector_tiles((outer * (1.0 / math.sqrt(acts.shape[1]))).astype(BF16))
+    start_test_blocks()
+    pass_vector_tiles(0)
+    pass_vector_tiles(1)
+
+    other = 1 - core
     copies = []
-
-    def forward(i, rows):
-        copies.append(core_copy(i, rows))
-        copies[-1].start()
-
     for dy in (0, 1, 3, 2):
-        if dy == 2:
-            place_cross(0)
-            forward(0, v_all.at[core, :, :, pl.ds(SPLIT, (CHUNKS - ACROSS) * 128)])
-        first = lax.rem(y + NY - dy, NY) * NX
-        count = NX - (dy == 0)
-        await_bytes(v_all.at[core, pl.ds(first, count), :, pl.ds(0, SPLIT)], rows_recv.at[dy])
-        forward(dy + 1, v_all.at[core, pl.ds(first, NX), :, pl.ds(0, SPLIT)])
-    for copy in copies:
+        first = group_start(dy)
+        await_bytes(tiles.at[core, pl.ds(first, NX - (dy == 0))], v_recv.at[2 + dy])
+        copies.append(core_copy(dy, tiles.at[core, pl.ds(first, NX)]))
+        if dy != 2:
+            lay_out(core, dy)
+    for copy, dy in zip(copies, (0, 1, 3)):
         copy.wait_recv()
+        lay_out(other, dy)
+    lay_out(core, 2)
+    place_test_blocks()
+    copies.append(core_copy(NY, t_all.at[core]))
+    copies[NY - 1].wait_recv()
+    lay_out(other, 2)
 
     small[5].wait()
     v = v_all[...].reshape(2 * HALF, -1)
     top = approximate_inverse(v, split_ref, m_ref)
-    place_cross(1)
-    await_bytes(t_all.at[core, pl.ds(0, STEPS), :, pl.ds(0, SPLIT)], rows_recv.at[NY])
-    forward(NY + 1, t_all.at[core])
     sol, excess = refined(wanted_rows(ids_ref, 2 * HALF), top, split_ref, m_ref)
     copies[-1].wait_recv()
     raw_ref[...] = scores_of(sol, v, t_all[...].reshape(2 * HALF, -1))
     check_ref[...] = jnp.broadcast_to(excess, check_ref.shape)
-    for a in range(2):
-        await_bytes(line.at[a, pl.ds(0, NZ - 1)], line_send.at[a])
-        await_bytes(plane.at[a, pl.ds(0, STEPS)], plane_send.at[a])
-        await_bytes(fulls[a].at[core, pl.ds(0, STEPS), :, pl.ds(0, SPLIT)], rows_send.at[a])
-        await_bytes(cross.at[a, pl.ds(0, NZ - 1)], cross_send.at[a])
+    await_bytes(line.at[pl.ds(0, NZ - 1)], line_send)
+    await_bytes(plane.at[pl.ds(0, STEPS)], plane_send)
+    await_bytes(t_all.at[core, pl.ds(0, STEPS), :, pl.ds(0, SPLIT)], rows_send)
+    await_bytes(cross.at[pl.ds(0, NZ - 1)], cross_send)
+    await_bytes(tiles.at[core, mine, pl.ds(0, NZ - 1)], v_send.at[0])
+    await_bytes(tiles.at[core, pl.ds(0, STEPS)], v_send.at[1])
     for copy in copies:
         copy.wait_send()
 
@@ -471,27 +503,20 @@
             like(proj_in),
             like(proj_out),
             like(test_grads),
-            pltpu.VMEM((2, TILE, 128), BF16),
-            pltpu.VMEM((2, NZ, TILE, 128), BF16),
-            pltpu.VMEM((2, PLANE, TILE, 128), BF16),
-            pltpu.VMEM((2, NZ, 2 * PLANE, (CHUNKS - ACROSS) * 128), BF16),
-            pltpu.VMEM((PLANE * TILE, 128), F32),
+            pltpu.VMEM((2, PLANE, NZ, TILE, 128), BF16),
+            pltpu.VMEM((TILE, 128), BF16),
+            pltpu.VMEM((NZ, TILE, 128), BF16),
+            pltpu.VMEM((PLANE, TILE, 128), BF16),
+            pltpu.VMEM((NZ, 2 * PLANE, (CHUNKS - ACROSS) * 128), BF16),
+            pltpu.VMEM((NX * NZ * TILE, 128), F32),
             pltpu.VMEM((count, 3 * count), BF16),
             pltpu.VMEM((count, count), BF16),
             dma((6,)),
             dma((PARTS,)),
             dma((PARTS,)),
-            dma((2,)),
-            dma((2,)),
-            dma((2,)),
-            dma((2,)),
-            dma((2,)),
-            dma((NY + 1,)),
-            dma((2,)),
-            dma((2,)),
-            dma((NY + 2,)),
-            dma((NY + 2,)),
-        ],
+        ]
+        + [dma] * 8
+        + [dma((2,)), dma((2 + NY,)), dma((NY + 1,)), dma((NY + 1,))],
         compiler_params=pltpu.CompilerParams(
             collective_id=0, has_side_effects=True, vmem_limit_bytes=56 << 20
         ),

time: 62.4 us -> 64.1 us (1.027)
  the two profiles are of different devices: /device:TPU:25 before, /device:TPU:3 now
where the time goes in v6:
time: 64.1 us
  Pallas kernels  64.1 us (100%)
    pallas_call x1, Pallas kernels, body(): pl.pallas_call(main_kernel, out_shape=(pltpu.VMEM((8, count), F32), pltpu...  35.2 us
    pallas_call x1, Pallas kernels, body(): pl.pallas_call(finish_kernel, out_shape=jax.ShapeDtypeStruct((2, count),...  28.9 us

profile of v6, /device:TPU:3, one launch (start us, length us, event | category | flops | bytes accessed | tf_op | source)
XLA Modules:
  0.0 64.1 jit_solution(10466928692941227896)
XLA Ops:
  0.0 0.0 copy-start
  0.0 35.2 %shard_map.82 = (f32[8,512]{1,0:T(8,128)S(1)}, f32[8,128]{1,0:T(8,128)S(1)}, bf16[2,16,16,1024]{3,2,1,0:T(8,128)(2,1)S(1)}, bf16[2,16,16,1024]{3,2,1,0:T(8,128)(2,1)S(1)}) custom-call(s32[2]{0:T(128)} %ids_ref.1, bf16[2,64,768]{2,1,0:T(8,128)(2,1)} %acts_hbm.1, bf16[2,64,768]{2,1,0:T(8,128)(2,1)} %cot_hbm.1, bf16[768,3072]{1,0:T(8,128)(2,1)} %w_in_hbm.1, ...), custom_call_target="tpu_custom_call" | custom-call | tf_op jit(solution)/shard_map/pallas_call | solution.py:487
  35.2 0.0 copy-done
  35.2 28.9 %shard_map.83 = f32[2,512]{1,0:T(2,128)} custom-call(s32[2]{0:T(128)S(1)} %copy-done, f32[8,512]{1,0:T(8,128)S(1)} %get-tuple-element.9.raw_ref, f32[8,128]{1,0:T(8,128)S(1)} %get-tuple-element.10.check_ref, bf16[2,16,16,1024]{3,2,1,0:T(8,128)(2,1)S(1)} %get-tuple-element.11.v_ref, bf16[2,16,16,1024]{3,2,1,0:T(8,128)(2,1)S(1)} %get-tuple-element.12.t_ref), custom_call_target="tpu_custom_call" | custom-call | tf_op jit(solution)/shard_map/pallas_call | solution.py:533
Async XLA Ops:
  0.0 35.2 %copy-start = (s32[2]{0:T(128)S(1)}, s32[2]{0:T(128)}, u32[]{:S(2)}) copy-start(s32[2]{0:T(128)} %ids_ref.1) | copy-start | bytes 28

commit v7 on v5

--- a/solution.py
+++ b/solution.py
@@ -30,8 +30,8 @@
 STEPS = len(PLANE_STEPS)
 LINE_STEPS = sorted(range(1, NZ), key=lambda d: -min(d, NZ - d))
 CHUNKS = 8
-ACROSS = 6
-SPLIT = ACROSS * 128
+ACROSS = (6, 6)
+SPLIT = (ACROSS[0] * 128, ACROSS[1] * 128)
 
 
 def gelu_slope(values):
@@ -160,18 +160,19 @@
     return system, damping, diagonal + damping, eye
 
 
-def times_system(p, split_ref):
+def times_system(p, split_ref, used=3):
     count = split_ref.shape[0]
-    product = unstacked(mm(stacked(p), split_ref[...]))
-    return (
-        product[:, 0:count] + product[:, count : 2 * count] + product[:, 2 * count : 3 * count]
-    )
-
-
-def scores_of(sol, v, t):
+    product = unstacked(mm(stacked(p), split_ref[:, 0 : used * count]))
+    total = product[:, 0:count]
+    for i in range(1, used):
+        total = total + product[:, i * count : (i + 1) * count]
+    return total
+
+
+def scores_of(sol, v, t, order):
     mixed = unstacked(mm(stacked(sol), v))
     raw = unstacked(mm_t(stacked(mixed), t)) * (1.0 / math.sqrt(v.shape[1]))
-    return unstacked(mm(stacked(raw), target_order((t.shape[0], t.shape[0]))))
+    return unstacked(mm(stacked(raw), order))
 
 
 def approximate_inverse(v, split_ref, m_ref):
@@ -204,10 +205,10 @@
         return mm(jnp.concatenate([r, jnp.zeros_like(r)], axis=0).astype(BF16), m_ref[...])[0:8]
 
     sol = precondition(rhs)
-    res = rhs - times_system(sol, split_ref)
-    for _ in range(REFINEMENTS):
+    res = rhs - times_system(sol, split_ref, 2)
+    for i in range(REFINEMENTS):
         sol = sol + precondition(res)
-        res = rhs - times_system(sol, split_ref)
+        res = rhs - times_system(sol, split_ref, 2 if i == 0 else 3)
     excess = inner(res, res) - (LAST_BITS * top) * (LAST_BITS * top) * inner(sol, sol)
     return sol, excess
 
@@ -216,7 +217,7 @@
     ids_hbm, acts_hbm, cot_hbm, w_in_hbm, w_out_hbm, proj_in_hbm, proj_out_hbm, test_hbm,
     raw_ref, check_ref, v_all, t_all,
     ids_ref, acts, cot, w_in, w_out, proj_in, proj_out, test,
-    tiles, line, plane, cross, wide, split_ref, m_ref,
+    tiles, line, plane, v_cross, t_cross, wide, split_ref, m_ref, order_ref,
     load_sem, in_sem, out_sem,
     line_send, line_recv, plane_send, plane_recv,
     rows_send, rows_recv, cross_send, cross_recv, core_send, core_recv,
@@ -269,7 +270,7 @@
     for target in targets:
         pl.semaphore_signal(barrier, inc=1, device_id=target, device_id_type=MESH)
 
-    fulls = (v_all, t_all)
+    fulls, crosses = (v_all, t_all), (v_cross, t_cross)
     mine = y * NX + x
 
     def send(src, dst, send_sem, recv_sem, target):
@@ -298,32 +299,33 @@
         full = fulls[a]
         await_bytes(line.at[a, pl.ds(0, NZ - 1)], line_recv.at[a])
         wide[0 : NZ * TILE, :] = line[a].reshape(NZ * TILE, 128).astype(F32)
-        for c in range(ACROSS):
+        for c in range(ACROSS[a]):
             both = [wide[pl.ds(k * CHUNKS + c, NZ, stride=TILE), :] for k in range(2)]
             full[core, mine, :, c * 128 : (c + 1) * 128] = jnp.concatenate(both, axis=0).astype(
                 BF16
             )
-        rows = full.at[core, mine, :, pl.ds(0, SPLIT)]
+        rows = full.at[core, mine, :, pl.ds(0, SPLIT[a])]
         for (dy, _), target in zip(PLANE_STEPS, on_plane):
             send(rows, rows, rows_send.at[a], rows_recv.at[dy if a == 0 else NY], target)
         await_bytes(plane.at[a, pl.ds(0, STEPS)], plane_recv.at[a])
         wide[...] = plane[a].reshape(PLANE * TILE, 128).astype(F32)
-        for c in range(ACROSS, CHUNKS):
+        for c in range(ACROSS[a], CHUNKS):
             both = [wide[pl.ds(k * CHUNKS + c, PLANE, stride=TILE), :] for k in range(2)]
-            cross[a, z, :, (c - ACROSS) * 128 : (c - ACROSS + 1) * 128] = jnp.concatenate(
-                both, axis=0
-            ).astype(BF16)
-        rows = cross.at[a, z]
+            at = c - ACROSS[a]
+            crosses[a][z, :, at * 128 : (at + 1) * 128] = jnp.concatenate(both, axis=0).astype(BF16)
+        rows = crosses[a].at[z]
         for target in on_line:
             send(rows, rows, cross_send.at[a], cross_recv.at[a], target)
 
     def place_cross(a):
-        await_bytes(cross.at[a, pl.ds(0, NZ - 1)], cross_recv.at[a])
-        for c in range(CHUNKS - ACROSS):
-            wide[...] = cross[a, :, :, c * 128 : (c + 1) * 128].reshape(NZ * 2 * PLANE, 128).astype(F32)
+        await_bytes(crosses[a].at[pl.ds(0, NZ - 1)], cross_recv.at[a])
+        for c in range(ACROSS[a], CHUNKS):
+            at = c - ACROSS[a]
+            columns = crosses[a][:, :, at * 128 : (at + 1) * 128]
+            wide[...] = columns.reshape(NZ * 2 * PLANE, 128).astype(F32)
             for p in range(PLANE):
                 both = [wide[pl.ds(k * PLANE + p, NZ, stride=2 * PLANE), :] for k in range(2)]
-                fulls[a][core, p, :, SPLIT + c * 128 : SPLIT + (c + 1) * 128] = jnp.concatenate(
+                fulls[a][core, p, :, c * 128 : (c + 1) * 128] = jnp.concatenate(
                     both, axis=0
                 ).astype(BF16)
 
@@ -359,8 +361,9 @@
         right = term if right is None else right + term
     outer = outer_tile(left, right, proj_in.shape[0])
     start_tiles(0, (outer * (1.0 / math.sqrt(acts.shape[1]))).astype(BF16))
+    start_blocks(1)
     start_blocks(0)
-    start_blocks(1)
+    order_ref[...] = target_order(order_ref.shape)
 
     copies = []
 
@@ -371,37 +374,40 @@
     for dy in (0, 1, 3, 2):
         if dy == 2:
             place_cross(0)
-            forward(0, v_all.at[core, :, :, pl.ds(SPLIT, (CHUNKS - ACROSS) * 128)])
+            forward(0, v_all.at[core, :, :, pl.ds(SPLIT[0], (CHUNKS - ACROSS[0]) * 128)])
         first = lax.rem(y + NY - dy, NY) * NX
         count = NX - (dy == 0)
-        await_bytes(v_all.at[core, pl.ds(first, count), :, pl.ds(0, SPLIT)], rows_recv.at[dy])
-        forward(dy + 1, v_all.at[core, pl.ds(first, NX), :, pl.ds(0, SPLIT)])
-    for copy in copies:
+        await_bytes(v_all.at[core, pl.ds(first, count), :, pl.ds(0, SPLIT[0])], rows_recv.at[dy])
+        forward(dy + 1, v_all.at[core, pl.ds(first, NX), :, pl.ds(0, SPLIT[0])])
+    place_cross(1)
+    await_bytes(t_all.at[core, pl.ds(0, STEPS), :, pl.ds(0, SPLIT[1])], rows_recv.at[NY])
+    forward(NY + 1, t_all.at[core])
+    for copy in copies[:-1]:
         copy.wait_recv()
 
     small[5].wait()
     v = v_all[...].reshape(2 * HALF, -1)
     top = approximate_inverse(v, split_ref, m_ref)
-    place_cross(1)
-    await_bytes(t_all.at[core, pl.ds(0, STEPS), :, pl.ds(0, SPLIT)], rows_recv.at[NY])
-    forward(NY + 1, t_all.at[core])
     sol, excess = refined(wanted_rows(ids_ref, 2 * HALF), top, split_ref, m_ref)
     copies[-1].wait_recv()
-    raw_ref[...] = scores_of(sol, v, t_all[...].reshape(2 * HALF, -1))
+    raw = scores_of(sol, v, t_all[...].reshape(2 * HALF, -1), order_ref[...])
+    raw_ref[...] = raw[0:2]
     check_ref[...] = jnp.broadcast_to(excess, check_ref.shape)
     for a in range(2):
         await_bytes(line.at[a, pl.ds(0, NZ - 1)], line_send.at[a])
         await_bytes(plane.at[a, pl.ds(0, STEPS)], plane_send.at[a])
-        await_bytes(fulls[a].at[core, pl.ds(0, STEPS), :, pl.ds(0, SPLIT)], rows_send.at[a])
-        await_bytes(cross.at[a, pl.ds(0, NZ - 1)], cross_send.at[a])
+        await_bytes(fulls[a].at[core, pl.ds(0, STEPS), :, pl.ds(0, SPLIT[a])], rows_send.at[a])
+        await_bytes(crosses[a].at[pl.ds(0, NZ - 1)], cross_send.at[a])
     for copy in copies:
         copy.wait_send()
 
 
-def finish_kernel(ids_ref, raw_ref, check_ref, v_ref, t_ref, out_ref, split_ref):
-    out_ref[...] = raw_ref[0:2]
+def finish_kernel(ids_ref, raw_ref, check_ref, v_ref, t_ref, out_hbm, late_ref, split_ref, sem):
+    copy = pltpu.make_async_copy(raw_ref, out_hbm, sem)
+    copy.start()
     excess = check_ref[...]
     fine = jnp.min(jnp.where(excess <= 0.0, 1.0, 0.0))
+    copy.wait()
 
     @pl.when(fine < 1.0)
     def _():
@@ -434,7 +440,10 @@
         goal = rz * 1e-12
         state = (jnp.int32(0), jnp.zeros_like(rhs), rhs, zed, rz)
         sol = lax.while_loop(unfinished, advance, state)[1]
-        out_ref[...] = scores_of(sol, v, t)[0:2]
+        late_ref[...] = scores_of(sol, v, t, target_order((count, count)))[0:2]
+        again = pltpu.make_async_copy(late_ref, out_hbm, sem)
+        again.start()
+        again.wait()
 
 
 def body(
@@ -455,7 +464,7 @@
     raw, check, v_all, t_all = pl.pallas_call(
         main_kernel,
         out_shape=(
-            pltpu.VMEM((8, count), F32),
+            pltpu.VMEM((2, count), F32),
             pltpu.VMEM((8, 128), F32),
             pltpu.VMEM(full.shape, BF16),
             pltpu.VMEM(full.shape, BF16),
@@ -474,9 +483,11 @@
             pltpu.VMEM((2, TILE, 128), BF16),
             pltpu.VMEM((2, NZ, TILE, 128), BF16),
             pltpu.VMEM((2, PLANE, TILE, 128), BF16),
-            pltpu.VMEM((2, NZ, 2 * PLANE, (CHUNKS - ACROSS) * 128), BF16),
+            pltpu.VMEM((NZ, 2 * PLANE, (CHUNKS - ACROSS[0]) * 128), BF16),
+            pltpu.VMEM((NZ, 2 * PLANE, (CHUNKS - ACROSS[1]) * 128), BF16),
             pltpu.VMEM((PLANE * TILE, 128), F32),
             pltpu.VMEM((count, 3 * count), BF16),
+            pltpu.VMEM((count, count), BF16),
             pltpu.VMEM((count, count), BF16),
             dma((6,)),
             dma((PARTS,)),
@@ -509,9 +520,11 @@
         finish_kernel,
         out_shape=jax.ShapeDtypeStruct((2, count), F32),
         in_specs=[smem, vmem, vmem, vmem, vmem],
-        out_specs=vmem,
+        out_specs=hbm,
         scratch_shapes=[
+            pltpu.VMEM((2, count), F32),
             pltpu.VMEM((count, 3 * count), BF16),
+            dma,
         ],
         compiler_params=pltpu.CompilerParams(vmem_limit_bytes=32 << 20),
     )(clip_ids, *[pltpu.with_memory_space_constraint(r, pltpu.VMEM) for r in (raw, check, v_all, t_all)])

time: 62.4 us -> 64.4 us (1.032)
  the two profiles are of different devices: /device:TPU:25 before, /device:TPU:1 now
where the time goes in v7:
time: 64.4 us; the launch traced here: 64.3 us
  Pallas kernels  64.3 us (100%)
    pallas_call x1, Pallas kernels, body(): pl.pallas_call(main_kernel, out_shape=(pltpu.VMEM((2, count), F32), pltpu...  34.9 us
    pallas_call x1, Pallas kernels, body(): pl.pallas_call(finish_kernel, out_shape=jax.ShapeDtypeStruct((2, count),...  29.4 us

profile of v7, /device:TPU:1, one launch (start us, length us, event | category | flops | bytes accessed | tf_op | source)
XLA Modules:
  0.0 64.3 jit_solution(13340629047682525411)
XLA Ops:
  0.0 0.0 copy-start
  0.0 34.9 %shard_map.82 = (f32[2,512]{1,0:T(2,128)S(1)}, f32[8,128]{1,0:T(8,128)S(1)}, bf16[2,16,16,1024]{3,2,1,0:T(8,128)(2,1)S(1)}, bf16[2,16,16,1024]{3,2,1,0:T(8,128)(2,1)S(1)}) custom-call(s32[2]{0:T(128)} %ids_ref.1, bf16[2,64,768]{2,1,0:T(8,128)(2,1)} %acts_hbm.1, bf16[2,64,768]{2,1,0:T(8,128)(2,1)} %cot_hbm.1, bf16[768,3072]{1,0:T(8,128)(2,1)} %w_in_hbm.1, ...), custom_call_target="tpu_custom_call" | custom-call | tf_op jit(solution)/shard_map/pallas_call | solution.py:464
  34.9 0.0 copy-done
  34.9 29.4 %shard_map.83 = f32[2,512]{1,0:T(2,128)} custom-call(s32[2]{0:T(128)S(1)} %copy-done, f32[2,512]{1,0:T(2,128)S(1)} %get-tuple-element.9.raw_ref, f32[8,128]{1,0:T(8,128)S(1)} %get-tuple-element.10.check_ref, bf16[2,16,16,1024]{3,2,1,0:T(8,128)(2,1)S(1)} %get-tuple-element.11.v_ref, bf16[2,16,16,1024]{3,2,1,0:T(8,128)(2,1)S(1)} %get-tuple-element.12.t_ref), custom_call_target="tpu_custom_call" | custom-call | tf_op jit(solution)/shard_map/pallas_call | solution.py:519
Async XLA Ops:
  0.0 34.9 %copy-start = (s32[2]{0:T(128)S(1)}, s32[2]{0:T(128)}, u32[]{:S(2)}) copy-start(s32[2]{0:T(128)} %ids_ref.1) | copy-start | bytes 28
